TPU v7x, 256 devices: a whole 4x4x8 slice. The times are simulated.
256 devices in a mesh: batch: 4 (over y_lo, core), marker: 8 (over z), space: 8 (over y_hi, x).
Axes of the slice: x: 4, y: 4 (y_hi: 2, y_lo: 2; y = y_hi * 2 + y_lo), z: 8, core: 2. Of those that a mesh axis runs over, the one named last changes fastest.
Arguments:
- tokens: bfloat16 [4, 512, 48, 512], P('batch', 'space', 'marker'), may hold values from -100 to 100, as said below
- gain_first: float32 [512], replicated, may hold values from 0.1 to 1.9
- w_qkv_space: bfloat16 [512, 1536], replicated, may hold values from -0.25 to 0.25
- w_out_space: bfloat16 [512, 512], replicated, may hold values from -0.25 to 0.25
- gain_second: float32 [512], replicated, may hold values from 0.1 to 1.9
- w_qkv_marker: bfloat16 [512, 1536], replicated, may hold values from -0.25 to 0.25
- w_out_marker: bfloat16 [512, 512], replicated, may hold values from -0.25 to 0.25
- upstream: bfloat16 [4, 512, 48, 512], P('batch', 'space', 'marker'), may hold values from -6 to 6
Outputs:
- d_tokens: bfloat16 [4, 512, 48, 512], P('batch', 'space', 'marker')
- g_qkv_space: float32 [512, 1536], P(('marker', 'space'))
- g_out_space: float32 [512, 512], P(('marker', 'space'))
- g_gain_first: float32 [512], P(('marker', 'space'))
- g_qkv_marker: float32 [512, 1536], P(('marker', 'space'))
- g_out_marker: float32 [512, 512], P(('marker', 'space'))
- g_gain_second: float32 [512], P(('marker', 'space'))
Inputs may be any that keep to these rules, and one draw needn't show every extreme that they name: `tokens`: tokens have scales that differ from token to token and from feature to feature.
All inputs are finite; a program needn't handle non-finite values.
Results may differ from a plain program's by a relative error of at most 0.035.
Values may be sent and summed in bfloat16 or wider, within the bound.
No kernel may reach another device: no remote copies, remote signals or barrier semaphores. Data moves between devices by JAX's collectives and lax.ppermute only.
A program may use at most 128 MiB of HBM per device.

v0:
```python
import math

import jax
import jax.numpy as jnp
from jax import lax
from jax.sharding import PartitionSpec as P

HD = 64


epsilon = 1e-06


def normalize(wide, gain):
    scale = lax.rsqrt(jnp.mean(wide * wide, axis=-1, keepdims=True) + epsilon)
    return wide * scale * gain


def unit_rows(values):
    scale = lax.rsqrt(jnp.mean(values * values, axis=-1, keepdims=True) + epsilon)
    return values * scale


def attend(packed):
    length = packed.shape[0]
    heads = packed.shape[-1] // (3 * HD)
    wide = packed.reshape(length, heads, 3, HD).astype(jnp.float32)
    query = unit_rows(wide[:, :, 0])
    keys = unit_rows(wide[:, :, 1])
    scores = jnp.einsum("qhe,khe->hqk", query, keys) / math.sqrt(HD)
    weights = jnp.exp(scores)
    weights = weights / jnp.sum(weights, axis=-1, keepdims=True)
    rounded = lax.optimization_barrier(weights.astype(jnp.bfloat16)).astype(jnp.float32)
    mixed = jnp.einsum("hqk,khe->qhe", rounded, wide[:, :, 2])
    return mixed.reshape(length, heads * HD).astype(jnp.bfloat16)


def spatial(packed):
    moved = jnp.moveaxis(packed, 2, 0)
    result = lax.map(jax.checkpoint(jax.vmap(attend)), moved)
    return jnp.moveaxis(result, 0, 2)


def crosswise(packed):
    return lax.map(jax.checkpoint(jax.vmap(attend)), packed)


def outer_sum(left, right):
    dims = tuple(range(left.ndim - 1))
    return lax.dot_general(
        left, right, ((dims, dims), ((), ())), preferred_element_type=jnp.float32
    )


def backward_dot(values, weight):
    return lax.dot_general(
        values, weight, (((values.ndim - 1,), (1,)), ((), ())), preferred_element_type=jnp.float32
    )


def on_device(
    tokens, gain_first, w_qkv_space, w_out_space, gain_second, w_qkv_marker, w_out_marker, upstream
):
    spaces = lax.axis_size("space")
    block = lax.axis_index("space")
    width = w_qkv_space.shape[1] // spaces
    wide_tokens = tokens.astype(jnp.float32)
    first_wide, first_back = jax.vjp(normalize, wide_tokens, gain_first)
    first = first_wide.astype(jnp.bfloat16)
    own_columns = lax.dynamic_slice_in_dim(w_qkv_space, block * width, width, 1)
    first_all = lax.all_gather(first, "space", axis=1, tiled=True)
    qkv_one = jnp.dot(first_all, own_columns, preferred_element_type=jnp.float32).astype(
        jnp.bfloat16
    )
    heads_local, spatial_back = jax.vjp(spatial, qkv_one)
    heads_one = lax.all_to_all(heads_local, "space", split_axis=1, concat_axis=3, tiled=True)
    middle = (
        wide_tokens + jnp.dot(heads_one, w_out_space, preferred_element_type=jnp.float32)
    ).astype(jnp.bfloat16)
    second_wide, second_back = jax.vjp(normalize, middle.astype(jnp.float32), gain_second)
    second = second_wide.astype(jnp.bfloat16)
    second_all = lax.all_to_all(second, "marker", split_axis=1, concat_axis=2, tiled=True)
    qkv_two = jnp.dot(second_all, w_qkv_marker, preferred_element_type=jnp.float32).astype(
        jnp.bfloat16
    )
    cross_local, cross_back = jax.vjp(crosswise, qkv_two)
    heads_two = lax.all_to_all(cross_local, "marker", split_axis=2, concat_axis=1, tiled=True)
    d_heads_two = backward_dot(upstream, w_out_marker).astype(jnp.bfloat16)
    g_out_marker = outer_sum(heads_two, upstream)
    d_cross = lax.all_to_all(d_heads_two, "marker", split_axis=1, concat_axis=2, tiled=True)
    d_qkv_two = cross_back(d_cross)[0]
    g_qkv_marker = outer_sum(second_all, d_qkv_two)
    d_second_local = backward_dot(d_qkv_two, w_qkv_marker).astype(jnp.bfloat16)
    d_second = lax.all_to_all(d_second_local, "marker", split_axis=2, concat_axis=1, tiled=True)
    d_mid_norm, r_second = second_back(d_second.astype(jnp.float32))
    d_middle = (upstream.astype(jnp.float32) + d_mid_norm).astype(jnp.bfloat16)
    g_out_space = outer_sum(heads_one, d_middle)
    d_heads_mine = backward_dot(d_middle, w_out_space).astype(jnp.bfloat16)
    d_heads_one = lax.all_to_all(d_heads_mine, "space", split_axis=3, concat_axis=1, tiled=True)
    d_qkv_one = spatial_back(d_heads_one)[0]
    d_qkv_back = lax.all_to_all(d_qkv_one, "space", split_axis=1, concat_axis=3, tiled=True)
    d_first = backward_dot(d_qkv_back, w_qkv_space).astype(jnp.bfloat16)
    column_grad = outer_sum(first_all, d_qkv_one)
    marker_share = lax.psum_scatter(
        column_grad.astype(jnp.bfloat16), "marker", scatter_dimension=0, tiled=True
    ).astype(jnp.float32)
    qkv_share = lax.all_to_all(
        marker_share.astype(jnp.bfloat16), "space", split_axis=0, concat_axis=1, tiled=True
    ).astype(marker_share.dtype)
    d_tok_norm, r_first = first_back(d_first.astype(jnp.float32))
    d_tokens = (d_middle.astype(jnp.float32) + d_tok_norm).astype(jnp.bfloat16)
    out_share, first_share, qkvm_share, outm_share, second_share = (
        lax.psum_scatter(g_out_space, ("marker", "space"), scatter_dimension=0, tiled=True),
        lax.psum_scatter(r_first, ("marker", "space"), scatter_dimension=0, tiled=True),
        lax.psum_scatter(g_qkv_marker, ("marker", "space"), scatter_dimension=0, tiled=True),
        lax.psum_scatter(g_out_marker, ("marker", "space"), scatter_dimension=0, tiled=True),
        lax.psum_scatter(r_second, ("marker", "space"), scatter_dimension=0, tiled=True),
    )
    totals = (
        lax.psum(qkv_share.astype(jnp.bfloat16), "batch").astype(jnp.float32),
        lax.psum(out_share.astype(jnp.bfloat16), "batch").astype(jnp.float32),
        lax.psum(first_share.astype(jnp.bfloat16), "batch").astype(jnp.float32),
        lax.psum(qkvm_share.astype(jnp.bfloat16), "batch").astype(jnp.float32),
        lax.psum(outm_share.astype(jnp.bfloat16), "batch").astype(jnp.float32),
        lax.psum(second_share.astype(jnp.bfloat16), "batch").astype(jnp.float32),
    )
    count = (
        tokens.shape[0]
        * lax.axis_size("batch")
        * tokens.shape[1]
        * spaces
        * tokens.shape[2]
        * lax.axis_size("marker")
    )
    factor = 1.0 / math.sqrt(count)
    return (
        d_tokens,
        totals[0] * factor,
        totals[1] * factor,
        totals[2] * factor,
        totals[3] * factor,
        totals[4] * factor,
        totals[5] * factor,
    )


def solution(mesh):
    in_specs = (
        P("batch", "space", "marker", None),
        P(),
        P(),
        P(),
        P(),
        P(),
        P(),
        P("batch", "space", "marker", None),
    )
    out_specs = (
        P("batch", "space", "marker", None),
        P(("marker", "space"), None),
        P(("marker", "space"), None),
        P(("marker", "space")),
        P(("marker", "space"), None),
        P(("marker", "space"), None),
        P(("marker", "space")),
    )
    return jax.shard_map(
        on_device, mesh=mesh, in_specs=in_specs, out_specs=out_specs, check_vma=False
    )
```

profile of v0, /device:TPU:1, one launch (start us, length us, event | category | flops | bytes accessed | tf_op | source)
XLA Modules:
  0.0 1908.0 jit_solution(4187103554096790044)
XLA Ops:
  10.4 72.3 %all-gather.2.cloned.1.call-done = bf16[1,512,6,512]{3,1,2,0:T(8,128)(2,1)} async-done(((bf16[1,64,6,512]{3,1,2,0:T(8,128)(2,1)}), bf16[1,512,6,512]{3,1,2,0:T(8,128)(2,1)}) %all-gather.2.cloned.1.call-update) | async-done | bytes 3145744 | tf_op jit(solution)/shard_map/all_gather | solution.py:71
  85.9 5.1 while.32
  104.1 7.5 all-to-all-done
  111.6 6.7 all-to-all-start.2
  127.2 7.7 all-to-all-done.2
  139.8 14.9 all-to-all-done.1
  158.0 4.1 reshape.727
  162.2 6.7 fusion.157
  174.6 7.0 reshape.722
  181.6 4.6 fusion.154
  208.9 6.5 reshape.723
  218.9 4.1 all-to-all-start.3
  255.4 5.0 all-to-all-start.7
  264.3 25.1 %while.33 = (s32[]{:T(128)}, bf16[6,1,512,192]{2,3,1,0:T(8,128)(2,1)S(1)}, bf16[6,1,512,192]{2,3,1,0:T(8,128)(2,1)}, bf16[6,1,512,64]{3,2,1,0:T(8,128)(2,1)}, s32[]{:T(128)}, /*index=5*/s32[]{:T(128)}) while((s32[]{:T(128)}, bf16[6,1,512,192]{2,3,1,0:T(8,128)(2,1)S(1)}, bf16[6,1,512,192]{2,3,1,0:T(8,128)(2,1)}, ...), condition=%wide.region_21.22_spmd, body=%wide.region_14.21_spmd.sunk | while | flops 173808128 | bytes 13176925 | solution.py:40
  298.3 4.2 convolution_bitcast_fusion.1
  302.5 25.6 %reduce-scatter.5.cloned.1.call-done = bf16[64,192]{1,0:T(8,128)(2,1)} async-done(((bf16[512,192]{1,0:T(8,128)(2,1)}), bf16[64,192]{1,0:T(8,128)(2,1)}) %reduce-scatter.5.cloned.1.call-update) | async-done | bytes 24592 | tf_op jit(solution)/shard_map/reduce_scatter | solution.py:104
  328.1 6.8 all-to-all-start.6
  341.5 4.5 all-to-all-start.5
  348.0 26.9 %all-to-all-done.5 = bf16[1,512,6,192]{3,2,0,1:T(8,128)(2,1)} async-done(((bf16[1,512,6,192]{3,2,0,1:T(8,128)(2,1)}), bf16[1,512,6,192]{3,2,0,1:T(8,128)(2,1)}, u32[]{:S(2)}, u32[]{:S(2)}) %all-to-all-start.5) | async-done | bytes 1179680 | tf_op jit(solution)/shard_map/all_to_all | solution.py:101
  382.3 151.0 %all-reduce.8 = (bf16[512]{0:T(512)(128)(2,1)S(1)}, bf16[512]{0:T(512)(128)(2,1)S(1)}) all-reduce(f32[512]{0:T(512)S(1)} %get-tuple-element.184, f32[512]{0:T(512)S(1)} %copy-done.30), channel_id=4, replica_groups=mesh['batch'=4,'marker'=8,'space'=8] {'marker','space'}, use_global_device_ids=true, to_apply=%region_28.29.clone | all-reduce | flops 1024 | bytes 6144
  534.6 115.0 %reduce-scatter.11.cloned.1.call-done = f32[8,512]{1,0:T(8,128)} async-done(((f32[512,512]{1,0:T(8,128)}), f32[8,512]{1,0:T(8,128)}) %reduce-scatter.11.cloned.1.call-update) | async-done | bytes 16400 | tf_op jit(solution)/shard_map/reduce_scatter | solution.py:116
  650.9 357.5 %reduce-scatter.7.cloned.1.call-done = f32[8,512]{1,0:T(8,128)} async-done(((f32[512,512]{1,0:T(8,128)}), f32[8,512]{1,0:T(8,128)}) %reduce-scatter.7.cloned.1.call-update) | async-done | bytes 16400 | tf_op jit(solution)/shard_map/reduce_scatter | solution.py:113
  1009.7 836.4 %reduce-scatter.9.cloned.1.call-done = f32[8,1536]{1,0:T(8,128)} async-done(((f32[512,1536]{1,0:T(8,128)}), f32[8,1536]{1,0:T(8,128)}) %reduce-scatter.9.cloned.1.call-update) | async-done | bytes 49168 | tf_op jit(solution)/shard_map/reduce_scatter | solution.py:115
  1848.6 44.7 %all-reduce.12.cloned.1.call-done = (bf16[8,1536]{1,0:T(8,128)(2,1)}, bf16[8,512]{1,0:T(8,128)(2,1)}, bf16[8]{0:T(256)(128)(2,1)}, bf16[8,1536]{1,0:T(8,128)(2,1...) async-done(((bf16[8,1536]{1,0:T(8,128)(2,1)}, bf16[8,512]{1,0:T(8,128)(2,1)}, bf16[8]{0:T(256)(128)(2,1)}, bf16[8,1536]{1,0:T(8,128)(2,1)}, bf16[8,512]{1,0:T(8,128)(2,1)}, ...) | async-done | bytes 65584 | tf_op jit(solution)/shard_map/psum | solution.py:120
  (330 shorter events, 171.6 us)
Async XLA Ops:
  7.2 75.6 %copy-start = (bf16[512,1536]{1,0:T(8,128)(2,1)S(1)}, bf16[512,1536]{1,0:T(8,128)(2,1)}, u32[]{:S(2)}) copy-start(bf16[512,1536]{1,0:T(8,128)(2,1)} %param.14) | copy-start | bytes 4718596
  7.2 75.6 %all-gather.2.cloned.1.call-start = ((), (), s32[]{:S(2)}) async-start(), calls=%async_computation.12 | async-start | bytes 3538944 | tf_op jit(solution)/shard_map/all_gather | solution.py:71
  91.1 4.1 copy-start.3
  95.2 6.4 copy-start.13
  98.1 13.4 all-to-all-start
  111.6 23.3 %all-to-all-start.2 = ((bf16[1,64,6,512]{3,2,0,1:T(8,128)(2,1)}), bf16[1,64,6,512]{3,2,0,1:T(8,128)(2,1)S(1)}, u32[]{:S(2)}, u32[]{:S(2)}) async-start(bf16[1,64,6,512]{3,2,0,1:T(8,128)(2,1)} %copy.162), calls=%async_computation.2 | async-start | bytes 1048576 | tf_op jit(solution)/shard_map/all_to_all | solution.py:90
  122.4 3.6 copy-start.27
  134.9 19.8 %all-to-all-start.1 = ((bf16[1,64,6,512]{3,2,0,1:T(8,128)(2,1)}), bf16[1,64,6,512]{3,2,0,1:T(8,128)(2,1)S(1)}, u32[]{:S(2)}, u32[]{:S(2)}) async-start(bf16[1,64,6,512]{3,2,0,1:T(8,128)(2,1)} %copy.158), calls=%async_computation.1 | async-start | bytes 1048576 | tf_op jit(solution)/shard_map/all_to_all | solution.py:82
  188.4 3.4 copy-start.11
  218.9 15.9 all-to-all-start.3
  233.3 5.8 copy-start.14
  239.2 56.5 %copy-start.9 = (bf16[1,64,6,512]{3,1,2,0:T(8,128)(2,1)}, bf16[1,64,6,512]{3,1,2,0:T(8,128)(2,1)S(1)}, u32[]{:S(2)}) copy-start(bf16[1,64,6,512]{3,1,2,0:T(8,128)(2,1)S(1)} %fusion.121) | copy-start | bytes 1179652
  243.6 11.8 all-to-all-start.4
  255.4 5.0 copy-start.12
  255.4 37.6 %all-to-all-start.7 = ((bf16[1,8,48,512]{3,1,0,2:T(8,128)(2,1)}), bf16[1,8,48,512]{3,1,0,2:T(8,128)(2,1)}, u32[]{:S(2)}, u32[]{:S(2)}) async-start(bf16[1,8,48,512]{3,1,0,2:T(8,128)(2,1)} %reshape.740), calls=%async_computation.10 | async-start | bytes 786432 | tf_op jit(solution)/shard_map/all_to_all | solution.py:87
  260.4 67.7 %reduce-scatter.5.cloned.1.call-start = ((), (), s32[]{:S(2)}) async-start(), calls=%async_computation.13 | async-start | bytes 294912 | tf_op jit(solution)/shard_map/reduce_scatter | solution.py:104
  293.0 356.6 %reduce-scatter.11.cloned.1.call-start = ((), (), s32[]{:S(2)}) async-start(), calls=%async_computation.16 | async-start | bytes 1064960 | tf_op jit(solution)/shard_map/reduce_scatter | solution.py:116
  295.6 712.7 %reduce-scatter.7.cloned.1.call-start = ((), (), s32[]{:S(2)}) async-start(), calls=%async_computation.14 | async-start | bytes 1064960 | tf_op jit(solution)/shard_map/reduce_scatter | solution.py:113
  298.2 1547.9 %reduce-scatter.9.cloned.1.call-start = ((), (), s32[]{:S(2)}) async-start(), calls=%async_computation.15 | async-start | bytes 3194880 | tf_op jit(solution)/shard_map/reduce_scatter | solution.py:115
  328.1 13.4 all-to-all-start.6
  341.5 4.5 copy-start.32
  341.5 33.5 %all-to-all-start.5 = ((bf16[1,512,6,192]{3,2,0,1:T(8,128)(2,1)}), bf16[1,512,6,192]{3,2,0,1:T(8,128)(2,1)}, u32[]{:S(2)}, u32[]{:S(2)}) async-start(bf16[1,512,6,192]{3,2,0,1:T(8,128)(2,1)} %bitcast.409), calls=%async_computation.5 | async-start | bytes 4194304 | tf_op jit(solution)/shard_map/all_to_all | solution.py:101
  346.0 1547.3 %all-reduce.12.cloned.1.call-start = ((), (), s32[]{:S(2)}) async-start(), calls=%async_computation.17 | async-start | bytes 133120 | tf_op jit(solution)/shard_map/psum | solution.py:120
  380.1 1467.5 %copy-start.10 = (bf16[1,64,6,512]{3,1,2,0:T(8,128)(2,1)S(1)}, bf16[1,64,6,512]{3,1,2,0:T(8,128)(2,1)}, u32[]{:S(2)}) copy-start(bf16[1,64,6,512]{3,1,2,0:T(8,128)(2,1)} %copy-done.9) | copy-start | bytes 1179652
  (23 other events, 42.1 us)
Sparse Core Ops, SparseCore 0:
  11.2 71.5 all-gather.1
  293.1 34.9 reduce-scatter.4
  330.7 318.8 reduce-scatter.10
  651.9 356.4 reduce-scatter.6
  1014.7 831.2 reduce-scatter.8
  1849.6 43.5 all-reduce.11
where the time goes:
time: 1920 us; the launch traced here: 1910 us
  waiting for transfers between devices  1510 us (79%)
  blocking collectives  151 us (8%)
  local copies, waits for them, and re-layouts  94.3 us (5%)
  matrix products  49.3 us (3%)
  other arithmetic  43.8 us (2%)
  starting transfers between devices  38.2 us (2%)
    reduce_scatter x1, waiting for transfers between devices, on_device(): lax.psum_scatter(g_qkv_marker, ('marker', 'space'), scatter_dimension=0,...  836 us
    reduce_scatter x1, waiting for transfers between devices, on_device(): lax.psum_scatter(g_out_space, ('marker', 'space'), scatter_dimension=0, t...  357 us
    unnamed x1, blocking collectives  151 us
    reduce_scatter x1, waiting for transfers between devices, on_device(): lax.psum_scatter(g_out_marker, ('marker', 'space'), scatter_dimension=0,...  115 us
    all_gather x1, waiting for transfers between devices, on_device(): first_all = lax.all_gather(first, 'space', axis=1, tiled=True)  72.3 us
    psum x1, waiting for transfers between devices, on_device(): lax.psum(qkv_share.astype(jnp.bfloat16), 'batch').astype(jnp.float32)  44.7 us
  transfers between devices with their start and end apart: 14, of which 13 were waited for; matrix products, arithmetic and copies ran while one was open for 5% of the time, Pallas kernels for 0%

commit v1 on v0

v1 whole, which is shorter than its diff:
```python
import functools
import math

import jax
import jax.numpy as jnp
from jax import lax
from jax.experimental import pallas as pl
from jax.experimental.pallas import tpu as pltpu
from jax.sharding import PartitionSpec as P

HD = 64
EPS = 1e-06
BF = jnp.bfloat16
F32 = jnp.float32
LOG2E = math.log2(math.e)
VMEM_LIMIT = 56 * 1024 * 1024


def low_half(rows, width=128):
    return lax.broadcasted_iota(jnp.int32, (rows, width), 1) % 128 < HD


def swap(x):
    return pltpu.roll(x, HD, 1)


def dot(a, b):
    return jnp.dot(a, b, preferred_element_type=F32)


def dot_nt(a, b):
    return lax.dot_general(a, b, (((1,), (1,)), ((), ())), preferred_element_type=F32)


def half_mean(x, lo):
    first = jnp.sum(jnp.where(lo, x, 0.0), axis=-1, keepdims=True)
    second = jnp.sum(jnp.where(lo, 0.0, x), axis=-1, keepdims=True)
    return jnp.where(lo, first, second) * (1.0 / HD)


def half_scale(x, lo):
    return lax.rsqrt(half_mean(x * x, lo) + EPS)


def only_half(x, unit):
    own = x[unit * HD : (unit + 1) * HD]
    zero = jnp.zeros_like(own)
    return jnp.concatenate([own, zero] if unit == 0 else [zero, own], axis=0)


def row_scale(x):
    return lax.rsqrt(jnp.mean(x * x, axis=-1, keepdims=True) + EPS)


def norm_back(x, gain, cotangent):
    scale = row_scale(x)
    unit = x * scale
    pulled = cotangent * gain
    return scale * (pulled - unit * jnp.mean(pulled * unit, axis=-1, keepdims=True))


def scaled_pair(query, keys, lo):
    q_scale = half_scale(query, lo)
    k_scale = half_scale(keys, lo)
    return query * q_scale, q_scale, keys * k_scale, k_scale


def pair_back(d_qn, d_kn, qn, q_scale, kn, k_scale, lo):
    d_q = q_scale * (d_qn - qn * half_mean(d_qn * qn, lo))
    d_k = k_scale * (d_kn - kn * half_mean(d_kn * kn, lo))
    return d_q, d_k


def project_kernel(tokens_ref, gain_ref, w_ref, first_ref, send_ref):
    lo = low_half(64)
    x = tokens_ref[...].astype(F32)
    first = (x * row_scale(x) * gain_ref[...]).astype(BF)
    first_ref[...] = first
    for hh in range(4):
        wide = dot(first, w_ref[:, hh * 384 : (hh + 1) * 384])
        for jj in range(3):
            a = wide[(2 * jj) * 64 : (2 * jj + 1) * 64]
            b = wide[(2 * jj + 1) * 64 : (2 * jj + 2) * 64]
            for block in range(3):
                ba = a[:, block * 128 : (block + 1) * 128]
                bb = b[:, block * 128 : (block + 1) * 128]
                left = jnp.where(lo, ba, swap(bb)).astype(BF)
                right = jnp.where(lo, swap(ba), bb).astype(BF)
                for half, value in ((0, left), (1, right)):
                    part = 2 * block + half
                    head, kind = 2 * hh + part // 3, part % 3
                    at = jj * 384 + kind * 128
                    send_ref[head, :, at : at + 128] = value


def spatial_kernel(qkv_ref, heads_ref, inv_ref):
    length = qkv_ref.shape[0]
    lo = low_half(length)
    step = 256
    for jj in range(3):
        at = jj * 384
        query = qkv_ref[:, at : at + 128].astype(F32)
        keys = qkv_ref[:, at + 128 : at + 256].astype(F32)
        values = qkv_ref[:, at + 256 : at + 384].astype(F32)
        qn, _, kn, _ = scaled_pair(query, keys, lo)
        q_t = (qn * (LOG2E / 8.0)).T.astype(BF)
        kb = kn.astype(BF)
        v_t = values.T.astype(BF)
        out = []
        for unit in range(2):
            q_own = only_half(q_t, unit)
            cols = []
            for start in range(0, length, step):
                e = jnp.exp2(dot(kb, q_own[:, start : start + step]))
                inv = 1.0 / jnp.sum(e, axis=0, keepdims=True)
                inv_ref[2 * jj + unit : 2 * jj + unit + 1, start : start + step] = inv
                cols.append(dot(v_t[unit * HD : (unit + 1) * HD], e.astype(BF)) * inv)
            out.append(jnp.concatenate(cols, axis=1))
        heads_ref[:, jj * 128 : (jj + 1) * 128] = jnp.concatenate(out, axis=0).T.astype(BF)


def spatial_back_kernel(qkv_ref, heads_ref, inv_ref, d_heads_ref, d_qkv_ref):
    length = qkv_ref.shape[0]
    lo = low_half(length)
    step = 256
    for jj in range(3):
        at = jj * 384
        query = qkv_ref[:, at : at + 128].astype(F32)
        keys = qkv_ref[:, at + 128 : at + 256].astype(F32)
        vb = qkv_ref[:, at + 256 : at + 384]
        qn, q_scale, kn, k_scale = scaled_pair(query, keys, lo)
        qs = qn * (LOG2E / 8.0)
        q_t = qs.T.astype(BF)
        qb = qs.astype(BF)
        kb = kn.astype(BF)
        k_t = kn.T.astype(BF)
        o_t = heads_ref[:, jj * 128 : (jj + 1) * 128].astype(F32).T
        g_t = d_heads_ref[:, jj * 128 : (jj + 1) * 128].astype(F32).T
        scaled, drops = [], []
        for unit in range(2):
            rows = slice(unit * HD, (unit + 1) * HD)
            own = g_t[rows] * inv_ref[2 * jj + unit : 2 * jj + unit + 1, :]
            scaled.append(own)
            drops.append(jnp.sum(own * o_t[rows], axis=0, keepdims=True))
        g_scaled = jnp.concatenate(scaled, axis=0)
        gb = g_scaled.T.astype(BF)
        g_scaled = g_scaled.astype(BF)
        d_q, d_k, d_v = [], [], []
        for unit in range(2):
            q_own = only_half(q_t, unit)
            g_own = only_half(g_scaled, unit)
            cols, dk, dv = [], 0.0, 0.0
            for start in range(0, length, step):
                part = slice(start, start + step)
                e = jnp.exp2(dot(kb, q_own[:, part]))
                ds = (e * (dot(vb, g_own[:, part]) - drops[unit][:, part])).astype(BF)
                cols.append(dot(k_t[unit * HD : (unit + 1) * HD], ds))
                dk = dk + dot(ds, qb[part])
                dv = dv + dot(e.astype(BF), gb[part])
            d_q.append(jnp.concatenate(cols, axis=1))
            d_k.append(dk)
            d_v.append(dv)
        d_qn = jnp.concatenate(d_q, axis=0).T * (1.0 / 8.0)
        d_kn = jnp.where(lo, d_k[0], d_k[1]) * (1.0 / LOG2E)
        dq, dk = pair_back(d_qn, d_kn, qn, q_scale, kn, k_scale, lo)
        d_qkv_ref[:, at : at + 128] = dq.astype(BF)
        d_qkv_ref[:, at + 128 : at + 256] = dk.astype(BF)
        d_qkv_ref[:, at + 256 : at + 384] = jnp.where(lo, d_v[0], d_v[1]).astype(BF)


def middle_kernel(
    got_ref, tokens_ref, up_ref, w_out_ref, gain_ref, w_qkv_ref, w_last_ref,
    heads_one_ref, second_ref, d_qkv_ref, heads_two_ref, d_middle_ref, send_ref,
    qkv_ref, d_two_ref,
):
    lo64 = low_half(64)
    for hh in range(4):
        for jj in range(3):
            a = got_ref[2 * hh, :, jj * 128 : (jj + 1) * 128].astype(F32)
            b = got_ref[2 * hh + 1, :, jj * 128 : (jj + 1) * 128].astype(F32)
            cols = slice(hh * 128, (hh + 1) * 128)
            heads_one_ref[(2 * jj) * 64 : (2 * jj + 1) * 64, cols] = jnp.where(lo64, a, swap(b)).astype(BF)
            heads_one_ref[(2 * jj + 1) * 64 : (2 * jj + 2) * 64, cols] = jnp.where(lo64, swap(a), b).astype(BF)
    middle = tokens_ref[...].astype(F32) + dot(heads_one_ref[...], w_out_ref[...])
    middle = middle.astype(BF).astype(F32)
    gain = gain_ref[...]
    second = (middle * row_scale(middle) * gain).astype(BF)
    second_ref[...] = second
    qkv_ref[...] = dot(second, w_qkv_ref[...]).astype(BF)
    d_two_ref[...] = dot_nt(up_ref[...], w_last_ref[...]).astype(BF)

    length = qkv_ref.shape[0]
    lo = low_half(length)
    same = (
        lax.broadcasted_iota(jnp.int32, (length, length), 0) % 8
        == lax.broadcasted_iota(jnp.int32, (length, length), 1) % 8
    )
    for hh in range(4):
        at = hh * 384
        b0 = qkv_ref[:, at : at + 128].astype(F32)
        b1 = qkv_ref[:, at + 128 : at + 256].astype(F32)
        b2 = qkv_ref[:, at + 256 : at + 384].astype(F32)
        query = jnp.where(lo, b0, b1)
        keys = swap(jnp.where(lo, b2, b0))
        values = jnp.where(lo, b1, b2)
        qn, q_scale, kn, k_scale = scaled_pair(query, keys, lo)
        qs = qn * (LOG2E / 8.0)
        q_t = qs.T.astype(BF)
        qb = qs.astype(BF)
        kb = kn.astype(BF)
        k_t = kn.T.astype(BF)
        vb = values.astype(BF)
        v_t = values.T.astype(BF)
        g_t = d_two_ref[:, hh * 128 : (hh + 1) * 128].astype(F32).T
        o_t, d_q, d_k, d_v = [], [], [], []
        for unit in range(2):
            rows = slice(unit * HD, (unit + 1) * HD)
            e = jnp.where(same, jnp.exp2(dot(kb, only_half(q_t, unit))), 0.0)
            inv = 1.0 / jnp.sum(e, axis=0, keepdims=True)
            eb = e.astype(BF)
            o = dot(v_t[rows], eb) * inv
            own = g_t[rows] * inv
            drop = jnp.sum(own * o, axis=0, keepdims=True)
            zero = jnp.zeros_like(own)
            g_own = jnp.concatenate([own, zero] if unit == 0 else [zero, own], axis=0)
            gb = g_own.T.astype(BF)
            ds = (e * (dot(vb, g_own.astype(BF)) - drop)).astype(BF)
            o_t.append(o)
            d_q.append(dot(k_t[rows], ds))
            d_k.append(dot(ds, qb))
            d_v.append(dot(eb, gb))
        heads_two_ref[:, hh * 128 : (hh + 1) * 128] = jnp.concatenate(o_t, axis=0).T.astype(BF)
        d_qn = jnp.concatenate(d_q, axis=0).T * (1.0 / 8.0)
        d_kn = jnp.where(lo, d_k[0], d_k[1]) * (1.0 / LOG2E)
        dq, dk = pair_back(d_qn, d_kn, qn, q_scale, kn, k_scale, lo)
        dv = jnp.where(lo, d_v[0], d_v[1])
        dk = swap(dk)
        d_qkv_ref[:, at : at + 128] = jnp.where(lo, dq, dk).astype(BF)
        d_qkv_ref[:, at + 128 : at + 256] = jnp.where(lo, dv, dq).astype(BF)
        d_qkv_ref[:, at + 256 : at + 384] = jnp.where(lo, dk, dv).astype(BF)

    d_second = dot_nt(d_qkv_ref[...], w_qkv_ref[...]).astype(BF).astype(F32)
    d_middle = (up_ref[...].astype(F32) + norm_back(middle, gain, d_second)).astype(BF)
    d_middle_ref[...] = d_middle
    d_heads = dot_nt(d_middle, w_out_ref[...])
    for hh in range(4):
        for jj in range(3):
            a = d_heads[(2 * jj) * 64 : (2 * jj + 1) * 64, hh * 128 : (hh + 1) * 128]
            b = d_heads[(2 * jj + 1) * 64 : (2 * jj + 2) * 64, hh * 128 : (hh + 1) * 128]
            cols = slice(jj * 128, (jj + 1) * 128)
            send_ref[2 * hh, :, cols] = jnp.where(lo64, a, swap(b)).astype(BF)
            send_ref[2 * hh + 1, :, cols] = jnp.where(lo64, swap(a), b).astype(BF)


def last_kernel(got_ref, w_ref, tokens_ref, gain_ref, d_middle_ref, out_ref, d_qkv_ref):
    lo = low_half(64)
    for hh in range(4):
        for jj in range(3):
            part = []
            for head in (2 * hh, 2 * hh + 1):
                for kind in range(3):
                    at = jj * 384 + kind * 128
                    part.append(got_ref[head, :, at : at + 128].astype(F32))
            for block in range(3):
                left, right = part[2 * block], part[2 * block + 1]
                at = hh * 384 + block * 128
                d_qkv_ref[(2 * jj) * 64 : (2 * jj + 1) * 64, at : at + 128] = jnp.where(
                    lo, left, swap(right)
                ).astype(BF)
                d_qkv_ref[(2 * jj + 1) * 64 : (2 * jj + 2) * 64, at : at + 128] = jnp.where(
                    lo, swap(left), right
                ).astype(BF)
    d_first = dot_nt(d_qkv_ref[...], w_ref[...]).astype(BF).astype(F32)
    x = tokens_ref[...].astype(F32)
    out_ref[...] = (
        d_middle_ref[...].astype(F32) + norm_back(x, gain_ref[...], d_first)
    ).astype(BF)


def column_kernel(first_ref, d_qkv_ref, out_ref):
    lo = low_half(64, 384)
    total = jnp.zeros((512, 384), F32)
    for s in range(8):
        rows = []
        for jj in range(3):
            block = d_qkv_ref[s * 64 : (s + 1) * 64, jj * 384 : (jj + 1) * 384].astype(F32)
            rows.append(jnp.where(lo, block, 0.0).astype(BF))
            rows.append(jnp.where(lo, 0.0, block).astype(BF))
        total = total + dot(first_ref[s], jnp.concatenate(rows, axis=0))
    low = low_half(512)
    sums = [total[:, i * 128 : (i + 1) * 128] for i in range(3)]
    sums = [x + swap(x) for x in sums]
    out_ref[:, 0:128] = jnp.where(low, sums[0], sums[1]).astype(BF)
    out_ref[:, 128:192] = sums[2][:, :HD].astype(BF)


def call(kernel, outs, args, scratch=(), flops=10**9, moved=4 * 10**6, exps=0):
    return pl.pallas_call(
        kernel,
        out_shape=[jax.ShapeDtypeStruct(shape, dtype) for shape, dtype in outs],
        scratch_shapes=list(scratch),
        compiler_params=pltpu.CompilerParams(vmem_limit_bytes=VMEM_LIMIT),
        cost_estimate=pl.CostEstimate(flops=flops, bytes_accessed=moved, transcendentals=exps),
    )(*args)


def outer(left, right):
    return lax.dot_general(
        left, right, (((0,), (0,)), ((), ())), preferred_element_type=F32
    ).astype(BF)


def to_markers(x):
    lead = x.shape[:-2]
    k = len(lead)
    x = x.reshape(*lead, 6, 8, 8, 512)
    order = (k + 1, *range(k), k, k + 2, k + 3)
    x = jnp.transpose(x, order)
    x = lax.all_to_all(x, "marker", 0, 0, tiled=True)
    back = [0] * len(order)
    for i, o in enumerate(order):
        back[o] = i
    return jnp.transpose(x, back).reshape(*lead, 384, 512)


def swapped(x, bit):
    n = lax.axis_size("batch")
    return lax.ppermute(x, "batch", [(i, i ^ bit) for i in range(n)])


def halve(x, bit, shift):
    width = x.shape[1] // 2
    mine = (lax.axis_index("batch") >> shift) & 1
    keep = lax.dynamic_slice_in_dim(x, mine * width, width, 1)
    give = lax.dynamic_slice_in_dim(x, (1 - mine) * width, width, 1)
    return (keep.astype(F32) + swapped(give, bit).astype(F32)).astype(BF)


def on_device(
    tokens, gain_first, w_qkv_space, w_out_space, gain_second, w_qkv_marker, w_out_marker, upstream
):
    both = ("space", "marker")
    rows = ("marker", "space")
    mine = jnp.transpose(tokens[0], (1, 0, 2)).reshape(384, 512)
    up_mine = jnp.transpose(upstream[0], (1, 0, 2)).reshape(384, 512)
    gain_1 = gain_first.reshape(1, 512)
    gain_2 = gain_second.reshape(1, 512)

    first, qkv_send = call(
        project_kernel,
        [((384, 512), BF), ((8, 64, 1152), BF)],
        (mine, gain_1, w_qkv_space),
    )
    qkv_one = lax.all_to_all(qkv_send, "space", 0, 0, tiled=True).reshape(512, 1152)
    wide = to_markers(jnp.stack([mine, up_mine]))
    first_all = lax.all_gather(first.T, "space", axis=0, tiled=False)

    heads, inv = call(
        spatial_kernel, [((512, 384), BF), ((6, 512), F32)], (qkv_one,),
        flops=2 * 10**9, exps=6 * 512 * 512,
    )
    got = lax.all_to_all(heads, both, 0, 0, tiled=True).reshape(8, 64, 384)

    up_all = wide[1]
    heads_one, second, d_qkv_two, heads_two, d_middle, d_send = call(
        middle_kernel,
        [((384, 512), BF), ((384, 512), BF), ((384, 1536), BF), ((384, 512), BF),
         ((384, 512), BF), ((8, 64, 384), BF)],
        (got, wide[0], up_all, w_out_space, gain_2, w_qkv_marker, w_out_marker),
        scratch=[pltpu.VMEM((384, 1536), BF), pltpu.VMEM((384, 512), BF)],
        flops=6 * 10**9, exps=8 * 384 * 384,
    )
    d_heads = lax.all_to_all(d_send.reshape(512, 384), both, 0, 0, tiled=True)
    d_middle_mine = to_markers(d_middle)

    d_qkv_one, = call(
        spatial_back_kernel, [((512, 1152), BF)], (qkv_one, heads, inv, d_heads),
        flops=5 * 10**9, exps=6 * 512 * 512,
    )
    d_back = lax.all_to_all(d_qkv_one, "space", 0, 0, tiled=True).reshape(8, 64, 1152)
    d_tokens, = call(
        last_kernel, [((384, 512), BF)], (d_back, w_qkv_space, mine, gain_1, d_middle_mine),
        scratch=[pltpu.VMEM((384, 1536), BF)],
    )

    grads = jnp.concatenate(
        [outer(second, d_qkv_two), outer(heads_one, d_middle), outer(heads_two, up_all)], axis=1
    )
    share = halve(halve(grads, 1, 0), 2, 1)
    share = lax.all_to_all(share, rows, 0, 0, tiled=True)
    share = jnp.sum(share.reshape(64, 8, 640).astype(F32), axis=0).astype(BF)
    share = lax.all_gather(share, "batch", axis=0, tiled=False)
    share = share.reshape(2, 2, 8, 640).transpose(2, 1, 0, 3).reshape(8, 2560).astype(F32)

    column, = call(column_kernel, [((512, 192), BF)], (first_all, d_qkv_one), flops=2 * 10**9)
    column = lax.all_to_all(column, rows, 0, 0, tiled=True)
    column = jnp.sum(column.reshape(8, 8, 8, 192).astype(F32), axis=0)
    column = column.transpose(1, 0, 2).reshape(8, 1536).astype(BF)
    column = lax.all_gather(column, "batch", axis=0, tiled=False)
    column = jnp.sum(column.astype(F32), axis=0)

    count = 1
    for axis in ("batch", "marker", "space"):
        count *= lax.axis_size(axis)
    factor = 1.0 / math.sqrt(count * 384)
    at = (lax.axis_index("marker") * 8 + lax.axis_index("space")) * 8

    def gain_grad(weight, gain, grad):
        w = lax.dynamic_slice_in_dim(weight, at, 8, 0).astype(F32)
        return jnp.sum(w * grad, axis=1) / lax.dynamic_slice_in_dim(gain, at, 8, 0)

    g_qkv_space = column * factor
    g_qkv_marker = share[:, :1536] * factor
    return (
        jnp.transpose(d_tokens.reshape(6, 64, 512), (1, 0, 2))[None],
        g_qkv_space,
        share[:, 1536:2048] * factor,
        gain_grad(w_qkv_space, gain_first, g_qkv_space),
        g_qkv_marker,
        share[:, 2048:] * factor,
        gain_grad(w_qkv_marker, gain_second, g_qkv_marker),
    )


def solution(mesh):
    in_specs = (
        P("batch", "space", "marker", None),
        P(), P(), P(), P(), P(), P(),
        P("batch", "space", "marker", None),
    )
    shares = P(("marker", "space"), None)
    out_specs = (
        P("batch", "space", "marker", None),
        shares,
        shares,
        P(("marker", "space")),
        shares,
        shares,
        P(("marker", "space")),
    )
    return jax.shard_map(
        on_device, mesh=mesh, in_specs=in_specs, out_specs=out_specs, check_vma=False
    )
```

time: 1920 us -> 268 us (0.14)
  waiting for transfers between devices: 1510 us -> 115 us
  blocking collectives: 151 us -> 17 us
  local copies, waits for them, and re-layouts: 94.3 us -> 12.1 us
  matrix products: 49.3 us -> 4.38 us
  Pallas kernels: 0 us -> 38.1 us
  other arithmetic: 43.8 us -> 10.3 us
    reduce_scatter x4 -> x0, waiting for transfers between devices: 1330 us -> none  [the longest x1 836 us: on_device(): lax.psum_scatter(g_qkv_marker, ('marker', 'space'), scatter_dimension=0,...]
    unnamed x1 -> x0, blocking collectives: 151 us -> none
    all_gather x1, waiting for transfers between devices: 72.3 us -> 0.01 us  [on_device(): first_all = lax.all_gather(first.T, 'space', axis=0, tiled=False)]
    psum x1 -> x0, waiting for transfers between devices: 44.7 us -> none  [on_device(): lax.psum(qkv_share.astype(jnp.bfloat16), 'batch').astype(jnp.float32)]
    dot_general x59 -> x3, matrix products: 47.3 us -> 4.38 us  [outer(): lax.dot_general(left, right, (((0,), (0,)), ((), ())), preferred_element_...]
    pallas_call x0 -> x6, Pallas kernels: none -> 38.1 us  [call(): pl.pallas_call(kernel, out_shape=[jax.ShapeDtypeStruct(shape, dtype) for...]
    all_to_all x8, waiting for transfers between devices: 63 us -> 89.8 us  [the longest x2 19.6 us: to_markers(): x = lax.all_to_all(x, 'marker', 0, 0, tiled=True)]
    ppermute x0 -> x2, waiting for transfers between devices: none -> 24.5 us  [swapped(): return lax.ppermute(x, 'batch', [(i, i ^ bit) for i in range(n)])]
  transfers between devices with their start and end apart: 14 -> 11, of which waited for: 13 -> 8; matrix products, arithmetic and copies ran while one was open for 5% -> 7% of each run, Pallas kernels for 0% -> 11%
where the time goes in v1:
time: 268 us; the launch traced here: 267 us
  waiting for transfers between devices  115 us (43%)
  starting transfers between devices  55.8 us (21%)
  Pallas kernels  38.1 us (14%)
  blocking collectives  17 us (6%)
  between operations  14.3 us (5%)
  local copies, waits for them, and re-layouts  12.1 us (5%)
  other arithmetic  10.3 us (4%)
  matrix products  4.38 us (2%)
    pallas_call x6, Pallas kernels, call(): pl.pallas_call(kernel, out_shape=[jax.ShapeDtypeStruct(shape, dtype) for...  38.1 us
    ppermute x2, waiting for transfers between devices, swapped(): return lax.ppermute(x, 'batch', [(i, i ^ bit) for i in range(n)])  24.5 us
    all_to_all x2, waiting for transfers between devices, to_markers(): x = lax.all_to_all(x, 'marker', 0, 0, tiled=True)  19.6 us
    all_to_all x1, waiting for transfers between devices, on_device(): lax.all_to_all(qkv_send, 'space', 0, 0, tiled=True).reshape(512, 1152)  17.6 us
    all_to_all x1, waiting for transfers between devices, on_device(): d_heads = lax.all_to_all(d_send.reshape(512, 384), both, 0, 0, tiled=True)  15.3 us
    all_to_all x1, waiting for transfers between devices, on_device(): got = lax.all_to_all(heads, both, 0, 0, tiled=True).reshape(8, 64, 384)  13.4 us
    all_to_all x1, waiting for transfers between devices, on_device(): share = lax.all_to_all(share, rows, 0, 0, tiled=True)  13.3 us
    all_to_all x1, starting transfers between devices, on_device(): share = lax.all_to_all(share, rows, 0, 0, tiled=True)  13.3 us
  transfers between devices with their start and end apart: 11, of which 8 were waited for; matrix products, arithmetic and copies ran while one was open for 7% of the time, Pallas kernels for 11%

profile of v1, /device:TPU:1, one launch (start us, length us, event | category | flops | bytes accessed | tf_op | source)
XLA Modules:
  0.0 266.8 jit_solution(14825402809828050680)
XLA Ops:
  7.2 3.7 %shard_map.135 = (bf16[384,512]{1,0:T(8,128)(2,1)}, bf16[8,64,1152]{2,1,0:T(8,128)(2,1)}) custom-call(bf16[384,512]{1,0:T(8,128)(2,1)} %bitcast.55, f32[1,512]{1,0:T(1,128)} %bitcast.77, bf16[512,1536]{1,0:T(8,128)(2,1)} %w_ref.3), custom_call_target="tpu_custom_call" | custom-call | flops 1000000000 | bytes 4000000 | tf_op jit(solution)/shard_map/pallas_call | solution.py:298
  10.9 7.6 %all-to-all-start = ((bf16[8,64,1152]{2,1,0:T(8,128)(2,1)}), bf16[8,64,1152]{2,1,0:T(8,128)(2,1)S(1)}, u32[]{:S(2)}, u32[]{:S(2)}) async-start(bf16[8,64,1152]{2,1,0:T(8,128)(2,1)} %get-tuple-element.17), calls=%async_computation | async-start | bytes 2359296 | tf_op jit(solution)/shard_map/all_to_all | solution.py:354
  19.6 17.6 %all-to-all-done = bf16[8,64,1152]{2,1,0:T(8,128)(2,1)S(1)} async-done(((bf16[8,64,1152]{2,1,0:T(8,128)(2,1)}), bf16[8,64,1152]{2,1,0:T(8,128)(2,1)S(1)}, u32[]{:S(2)}, u32[]{:S(2)}) %all-to-all-start) | async-done | bytes 1179680 | tf_op jit(solution)/shard_map/all_to_all | solution.py:354
  37.2 8.2 %all-to-all-start.2 = ((bf16[8,2,6,8,512]{4,3,2,1,0:T(8,128)(2,1)}), bf16[8,2,6,8,512]{4,3,2,1,0:T(8,128)(2,1)S(1)}, u32[]{:S(2)}, u32[]{:S(2)}) async-start(bf16[8,2,6,8,512]{4,3,2,1,0:T(8,128)(2,1)} %copy.34), calls=%async_computation.2 | async-start | bytes 1572864 | tf_op jit(solution)/shard_map/all_to_all | solution.py:319
  45.4 5.8 %shard_map.136 = (bf16[512,384]{1,0:T(8,128)(2,1)}, f32[6,512]{1,0:T(8,128)}) custom-call(bf16[512,1152]{1,0:T(8,128)(2,1)} %bitcast.63), custom_call_target="tpu_custom_call" | custom-call | flops 2000000000 | bytes 4000000 | tf_op jit(solution)/shard_map/pallas_call | solution.py:298
  51.2 17.8 %all-to-all-done.2 = bf16[8,2,6,8,512]{4,3,2,1,0:T(8,128)(2,1)S(1)} async-done(((bf16[8,2,6,8,512]{4,3,2,1,0:T(8,128)(2,1)}), bf16[8,2,6,8,512]{4,3,2,1,0:T(8,128)(2,1)S(1)}, u32[]{:S(2)}, u32[]{:S(2)}) %all-to-all-start.2) | async-done | bytes 786464 | tf_op jit(solution)/shard_map/all_to_all | solution.py:319
  69.0 4.6 %all-to-all-start.1 = ((bf16[64,8,384]{2,1,0:T(8,128)(2,1)}), bf16[64,8,384]{2,1,0:T(8,128)(2,1)S(1)}, u32[]{:S(2)}, u32[]{:S(2)}) async-start(bf16[64,8,384]{2,1,0:T(8,128)(2,1)} %bitcast.69), calls=%async_computation.1 | async-start | bytes 786432 | tf_op jit(solution)/shard_map/all_to_all | solution.py:362
  76.0 13.4 %all-to-all-done.1 = bf16[64,8,384]{2,1,0:T(8,128)(2,1)S(1)} async-done(((bf16[64,8,384]{2,1,0:T(8,128)(2,1)}), bf16[64,8,384]{2,1,0:T(8,128)(2,1)S(1)}, u32[]{:S(2)}, u32[]{:S(2)}) %all-to-all-start.1) | async-done | bytes 393248 | tf_op jit(solution)/shard_map/all_to_all | solution.py:362
  90.2 11.6 %shard_map.137 = (bf16[384,512]{1,0:T(8,128)(2,1)}, bf16[384,512]{1,0:T(8,128)(2,1)}, bf16[384,1536]{1,0:T(8,128)(2,1)}, bf16[384,512]{1,0:T(8,128)(2,1)}, bf16[...) custom-call(bf16[8,64,384]{2,1,0:T(8,128)(2,1)} %bitcast.70, bf16[384,512]{1,0:T(8,128)(2,1)} %bitcast.72, ...), custom_call_target="tpu_custom_call" | custom-call | flops 6000000000 | bytes 4000000 | tf_op jit(solution)/shard_map/pallas_call | solution.py:298
  110.2 4.6 %all-to-all-start.3 = ((bf16[64,8,384]{2,1,0:T(8,128)(2,1)}), bf16[64,8,384]{2,1,0:T(8,128)(2,1)S(1)}, u32[]{:S(2)}, u32[]{:S(2)}) async-start(bf16[64,8,384]{2,1,0:T(8,128)(2,1)} %bitcast.17), calls=%async_computation.3 | async-start | bytes 786432 | tf_op jit(solution)/shard_map/all_to_all | solution.py:373
  115.7 15.3 %all-to-all-done.3 = bf16[64,8,384]{2,1,0:T(8,128)(2,1)S(1)} async-done(((bf16[64,8,384]{2,1,0:T(8,128)(2,1)}), bf16[64,8,384]{2,1,0:T(8,128)(2,1)S(1)}, u32[]{:S(2)}, u32[]{:S(2)}) %all-to-all-start.3) | async-done | bytes 393248 | tf_op jit(solution)/shard_map/all_to_all | solution.py:373
  131.0 4.1 %all-to-all-start.5 = ((bf16[8,6,8,512]{3,2,1,0:T(8,128)(2,1)}), bf16[8,6,8,512]{3,2,1,0:T(8,128)(2,1)S(1)}, u32[]{:S(2)}, u32[]{:S(2)}) async-start(bf16[8,6,8,512]{3,2,1,0:T(8,128)(2,1)} %bitcast.52), calls=%async_computation.5 | async-start | bytes 786432 | tf_op jit(solution)/shard_map/all_to_all | solution.py:319
  135.2 8.2 %shard_map.138.d_qkv_ref = bf16[512,1152]{1,0:T(8,128)(2,1)} custom-call(bf16[512,1152]{1,0:T(8,128)(2,1)} %bitcast.64, bf16[512,384]{1,0:T(8,128)(2,1)} %get-tuple-element.18.heads_ref, f32[6,512]{1,0:T(8,128)} %get-tuple-element.19.inv_ref, bf16[512,384]{1,0:T(8,128)(2,1)} %bitcast.71), custom_call_target="tpu_custom_call" | custom-call | flops 5000000000 | bytes 4000000 | tf_op jit(solution)/shard_map/pallas_call | solution.py:298
  147.9 3.6 %all-to-all-start.4 = ((bf16[8,64,1152]{2,1,0:T(8,128)(2,1)}), bf16[8,64,1152]{2,1,0:T(8,128)(2,1)S(1)}, u32[]{:S(2)}, u32[]{:S(2)}) async-start(bf16[8,64,1152]{2,1,0:T(8,128)(2,1)} %bitcast.65), calls=%async_computation.4 | async-start | bytes 2359296 | tf_op jit(solution)/shard_map/all_to_all | solution.py:380
  153.3 24.5 %collective-permute-done.1 = bf16[512,640]{1,0:T(8,128)(2,1)S(1)} collective-permute-done((bf16[512,640]{1,0:T(8,128)(2,1)}, bf16[512,640]{1,0:T(8,128)(2,1)S(1)}, u32[]{:S(2)}, u32[]{:S(2)}) %collective-permute-start.1) | collective-permute-done | bytes 655392 | tf_op jit(solution)/shard_map/ppermute | solution.py:328
  178.8 13.3 %all-to-all-start.7 = ((bf16[64,8,640]{2,1,0:T(8,128)(2,1)}), bf16[64,8,640]{2,1,0:T(8,128)(2,1)S(1)}, u32[]{:S(2)}, u32[]{:S(2)}) async-start(bf16[64,8,640]{2,1,0:T(8,128)(2,1)} %fusion), calls=%async_computation.7 | async-start | bytes 1310720 | tf_op jit(solution)/shard_map/all_to_all | solution.py:390
  193.0 3.7 %shard_map.139 = bf16[384,512]{1,0:T(8,128)(2,1)} custom-call(bf16[8,64,1152]{2,1,0:T(8,128)(2,1)} %copy-done.1, bf16[512,1536]{1,0:T(8,128)(2,1)} %w_ref.3, bf16[384,512]{1,0:T(8,128)(2,1)} %bitcast.56, f32[1,512]{1,0:T(1,128)} %bitcast.78, bf16[384,512]{1,0:T(8,128)(2,1)} %bitcast.59), custom_call_target="tpu_custom_call" | custom-call | flops 1000000000 | bytes 4000000 | tf_op jit(solution)/shard_map/pallas_call | solution.py:298
  196.7 13.3 %all-to-all-done.7 = bf16[64,8,640]{2,1,0:T(8,128)(2,1)S(1)} async-done(((bf16[64,8,640]{2,1,0:T(8,128)(2,1)}), bf16[64,8,640]{2,1,0:T(8,128)(2,1)S(1)}, u32[]{:S(2)}, u32[]{:S(2)}) %all-to-all-start.7) | async-done | bytes 655392 | tf_op jit(solution)/shard_map/all_to_all | solution.py:390
  210.1 9.7 %all-gather.1 = bf16[32,640]{1,0:T(8,128)(2,1)S(1)} all-gather(bf16[8,640]{1,0:T(8,128)(2,1)S(1)} %reduce_sum.50), channel_id=3, replica_groups=mesh['batch'=4,'marker'=8,'space'=8] {'batch'}, dimensions={0}, use_global_device_ids=true | all-gather | bytes 51200 | tf_op jit(solution)/shard_map/all_gather | solution.py:392
  221.4 4.7 %copy.39 = bf16[4096,384]{1,0:T(8,128)(2,1)} copy(bf16[4096,384]{0,1:T(8,128)(2,1)} %all-gather.4.cloned.1.call-done) | data formatting | bytes 6291456 | tf_op jit(solution)/shard_map/all_gather | solution.py:356
  226.1 5.1 %shard_map.140 = bf16[512,192]{1,0:T(8,128)(2,1)} custom-call(bf16[8,512,384]{2,1,0:T(8,128)(2,1)} %bitcast.53, bf16[512,1152]{1,0:T(8,128)(2,1)} %shard_map.138.d_qkv_ref), custom_call_target="tpu_custom_call" | custom-call | flops 2000000000 | bytes 4000000 | tf_op jit(solution)/shard_map/pallas_call | solution.py:298
  231.2 6.0 %all-to-all-start.6 = ((bf16[64,8,192]{2,1,0:T(8,128)(2,1)}), bf16[64,8,192]{2,1,0:T(8,128)(2,1)S(1)}, u32[]{:S(2)}, u32[]{:S(2)}) async-start(bf16[64,8,192]{2,1,0:T(8,128)(2,1)} %bitcast.74), calls=%async_computation.6 | async-start | bytes 524288 | tf_op jit(solution)/shard_map/all_to_all | solution.py:396
  239.2 10.5 %all-to-all-done.6 = bf16[64,8,192]{2,1,0:T(8,128)(2,1)S(1)} async-done(((bf16[64,8,192]{2,1,0:T(8,128)(2,1)}), bf16[64,8,192]{2,1,0:T(8,128)(2,1)S(1)}, u32[]{:S(2)}, u32[]{:S(2)}) %all-to-all-start.6) | async-done | bytes 196640 | tf_op jit(solution)/shard_map/all_to_all | solution.py:396
  249.8 7.4 %all_gather.18 = bf16[4,8,1536]{2,1,0:T(8,128)(2,1)S(1)} all-gather(bf16[1,8,1536]{2,1,0:T(8,128)(2,1)S(1)} %convert_element_type.76), channel_id=1, replica_groups=mesh['batch'=4,'marker'=8,'space'=8] {'batch'}, dimensions={0}, use_global_device_ids=true | all-gather | bytes 122880 | tf_op jit(solution)/shard_map/all_gather | solution.py:399
  (56 shorter events, 28.1 us)
Async XLA Ops:
  10.9 7.6 %copy-start.2 = (bf16[1,64,6,512]{3,1,2,0:T(8,128)(2,1)S(1)}, bf16[1,64,6,512]{3,1,2,0:T(8,128)(2,1)}, u32[]{:S(2)}) copy-start(bf16[1,64,6,512]{3,1,2,0:T(8,128)(2,1)} %param.8) | copy-start | bytes 1179652
  10.9 7.6 %copy-start.8 = (bf16[1,64,6,512]{3,1,2,0:T(8,128)(2,1)S(1)}, bf16[1,64,6,512]{3,1,2,0:T(8,128)(2,1)}, u32[]{:S(2)}) copy-start(bf16[1,64,6,512]{3,1,2,0:T(8,128)(2,1)} %param.15) | copy-start | bytes 1179652
  10.9 26.3 %all-to-all-start = ((bf16[8,64,1152]{2,1,0:T(8,128)(2,1)}), bf16[8,64,1152]{2,1,0:T(8,128)(2,1)S(1)}, u32[]{:S(2)}, u32[]{:S(2)}) async-start(bf16[8,64,1152]{2,1,0:T(8,128)(2,1)} %get-tuple-element.17), calls=%async_computation | async-start | bytes 2359296 | tf_op jit(solution)/shard_map/all_to_all | solution.py:354
  37.2 8.2 %copy-start.5 = (bf16[8,64,1152]{2,1,0:T(8,128)(2,1)}, bf16[8,64,1152]{2,1,0:T(8,128)(2,1)S(1)}, u32[]{:S(2)}) copy-start(bf16[8,64,1152]{2,1,0:T(8,128)(2,1)S(1)} %all-to-all-done) | copy-start | bytes 3538948
  37.2 31.8 %all-to-all-start.2 = ((bf16[8,2,6,8,512]{4,3,2,1,0:T(8,128)(2,1)}), bf16[8,2,6,8,512]{4,3,2,1,0:T(8,128)(2,1)S(1)}, u32[]{:S(2)}, u32[]{:S(2)}) async-start(bf16[8,2,6,8,512]{4,3,2,1,0:T(8,128)(2,1)} %copy.34), calls=%async_computation.2 | async-start | bytes 1572864 | tf_op jit(solution)/shard_map/all_to_all | solution.py:319
  69.0 20.4 %all-to-all-start.1 = ((bf16[64,8,384]{2,1,0:T(8,128)(2,1)}), bf16[64,8,384]{2,1,0:T(8,128)(2,1)S(1)}, u32[]{:S(2)}, u32[]{:S(2)}) async-start(bf16[64,8,384]{2,1,0:T(8,128)(2,1)} %bitcast.69), calls=%async_computation.1 | async-start | bytes 786432 | tf_op jit(solution)/shard_map/all_to_all | solution.py:362
  73.6 147.8 %all-gather.4.cloned.1.call-start = ((), (), s32[]{:S(2)}) async-start(), calls=%async_computation.8 | async-start | bytes 3538944 | tf_op jit(solution)/shard_map/all_gather | solution.py:356
  89.4 0.8 copy-start.6
  90.2 11.6 %copy-start.4 = (bf16[1,6,8,8,512]{4,3,2,1,0:T(8,128)(2,1)S(1)}, bf16[1,6,8,8,512]{4,3,2,1,0:T(8,128)(2,1)}, u32[]{:S(2)}) copy-start(bf16[1,6,8,8,512]{4,3,2,1,0:T(8,128)(2,1)} %copy.36) | copy-start | bytes 1179652
  103.2 2.5 copy-start.3
  103.2 2.5 copy-start.9
  107.6 35.9 %collective-permute-start = (bf16[512,1280]{1,0:T(8,128)(2,1)}, bf16[512,1280]{1,0:T(8,128)(2,1)}, u32[]{:S(2)}, u32[]{:S(2)}) collective-permute-start(bf16[512,1280]{1,0:T(8,128)(2,1)} %constant_dynamic-slice_fusion.1), channel_id=1, source_target_pairs={{0,64},{64,0},{128,192},{192,128},{1,65},{65,1},{129,193},{193,129... | collective-permute-start | bytes 3932168 | tf_op jit(solution)/shard_map/ppermute | solution.py:328
  110.2 20.8 %all-to-all-start.3 = ((bf16[64,8,384]{2,1,0:T(8,128)(2,1)}), bf16[64,8,384]{2,1,0:T(8,128)(2,1)S(1)}, u32[]{:S(2)}, u32[]{:S(2)}) async-start(bf16[64,8,384]{2,1,0:T(8,128)(2,1)} %bitcast.17), calls=%async_computation.3 | async-start | bytes 786432 | tf_op jit(solution)/shard_map/all_to_all | solution.py:373
  131.0 4.2 %copy-start.7 = (bf16[64,8,384]{2,1,0:T(8,128)(2,1)}, bf16[64,8,384]{2,1,0:T(8,128)(2,1)S(1)}, u32[]{:S(2)}) copy-start(bf16[64,8,384]{2,1,0:T(8,128)(2,1)S(1)} %all-to-all-done.3) | copy-start | bytes 1179652
  131.0 16.9 %all-to-all-start.5 = ((bf16[8,6,8,512]{3,2,1,0:T(8,128)(2,1)}), bf16[8,6,8,512]{3,2,1,0:T(8,128)(2,1)S(1)}, u32[]{:S(2)}, u32[]{:S(2)}) async-start(bf16[8,6,8,512]{3,2,1,0:T(8,128)(2,1)} %bitcast.52), calls=%async_computation.5 | async-start | bytes 786432 | tf_op jit(solution)/shard_map/all_to_all | solution.py:319
  146.2 5.4 %copy-start = (bf16[512,1280]{1,0:T(8,128)(2,1)S(1)}, bf16[512,1280]{1,0:T(8,128)(2,1)}, u32[]{:S(2)}) copy-start(bf16[512,1280]{1,0:T(8,128)(2,1)} %add_convert_fusion) | copy-start | bytes 3932164
  147.9 30.9 %all-to-all-start.4 = ((bf16[8,64,1152]{2,1,0:T(8,128)(2,1)}), bf16[8,64,1152]{2,1,0:T(8,128)(2,1)S(1)}, u32[]{:S(2)}, u32[]{:S(2)}) async-start(bf16[8,64,1152]{2,1,0:T(8,128)(2,1)} %bitcast.65), calls=%async_computation.4 | async-start | bytes 2359296 | tf_op jit(solution)/shard_map/all_to_all | solution.py:380
  152.4 25.4 %collective-permute-start.1 = (bf16[512,640]{1,0:T(8,128)(2,1)}, bf16[512,640]{1,0:T(8,128)(2,1)S(1)}, u32[]{:S(2)}, u32[]{:S(2)}) collective-permute-start(bf16[512,640]{1,0:T(8,128)(2,1)} %constant_dynamic-slice_fusion), channel_id=1, source_target_pairs={{0,128},{64,192},{128,0},{192,64},{1,129},{65,193},{129,1},{193,65... | collective-permute-start | bytes 1966088 | tf_op jit(solution)/shard_map/ppermute | solution.py:328
  178.8 14.1 %copy-start.1 = (bf16[8,64,1152]{2,1,0:T(8,128)(2,1)}, bf16[8,64,1152]{2,1,0:T(8,128)(2,1)S(1)}, u32[]{:S(2)}) copy-start(bf16[8,64,1152]{2,1,0:T(8,128)(2,1)S(1)} %all-to-all-done.4.got_ref) | copy-start | bytes 3538948
  178.8 31.2 %all-to-all-start.7 = ((bf16[64,8,640]{2,1,0:T(8,128)(2,1)}), bf16[64,8,640]{2,1,0:T(8,128)(2,1)S(1)}, u32[]{:S(2)}, u32[]{:S(2)}) async-start(bf16[64,8,640]{2,1,0:T(8,128)(2,1)} %fusion), calls=%async_computation.7 | async-start | bytes 1310720 | tf_op jit(solution)/shard_map/all_to_all | solution.py:390
  231.2 18.4 %all-to-all-start.6 = ((bf16[64,8,192]{2,1,0:T(8,128)(2,1)}), bf16[64,8,192]{2,1,0:T(8,128)(2,1)S(1)}, u32[]{:S(2)}, u32[]{:S(2)}) async-start(bf16[64,8,192]{2,1,0:T(8,128)(2,1)} %bitcast.74), calls=%async_computation.6 | async-start | bytes 524288 | tf_op jit(solution)/shard_map/all_to_all | solution.py:396
Sparse Core Ops, SparseCore 0:
  76.9 76.5 all-gather.3

commit v2 on v1

--- a/solution.py
+++ b/solution.py
@@ -13,7 +13,8 @@
 BF = jnp.bfloat16
 F32 = jnp.float32
 LOG2E = math.log2(math.e)
-VMEM_LIMIT = 56 * 1024 * 1024
+SMALL = 24 * 1024 * 1024
+LARGE = 56 * 1024 * 1024
 
 
 def low_half(rows, width=128):
@@ -30,6 +31,12 @@
 
 def dot_nt(a, b):
     return lax.dot_general(a, b, (((1,), (1,)), ((), ())), preferred_element_type=F32)
+
+
+def outer(left, right):
+    return lax.dot_general(
+        left, right, (((0,), (0,)), ((), ())), preferred_element_type=F32
+    ).astype(BF)
 
 
 def half_mean(x, lo):
@@ -71,11 +78,11 @@
     return d_q, d_k
 
 
-def project_kernel(tokens_ref, gain_ref, w_ref, first_ref, send_ref):
+def project_kernel(tokens_ref, gain_ref, w_ref, first_t_ref, send_ref):
     lo = low_half(64)
     x = tokens_ref[...].astype(F32)
     first = (x * row_scale(x) * gain_ref[...]).astype(BF)
-    first_ref[...] = first
+    first_t_ref[...] = first.astype(F32).T.astype(BF)
     for hh in range(4):
         wide = dot(first, w_ref[:, hh * 384 : (hh + 1) * 384])
         for jj in range(3):
@@ -169,9 +176,9 @@
 
 
 def middle_kernel(
-    got_ref, tokens_ref, up_ref, w_out_ref, gain_ref, w_qkv_ref, w_last_ref,
-    heads_one_ref, second_ref, d_qkv_ref, heads_two_ref, d_middle_ref, send_ref,
-    qkv_ref, d_two_ref,
+    core_ref, got_ref, tokens_ref, up_ref, w_out_ref, gain_ref, w_qkv_ref, w_last_ref,
+    keep_ref, give_ref, d_middle_ref, send_ref,
+    grads_ref, heads_one_ref, second_ref, d_qkv_ref, heads_two_ref, qkv_ref, d_two_ref,
 ):
     lo64 = low_half(64)
     for hh in range(4):
@@ -250,6 +257,12 @@
             cols = slice(jj * 128, (jj + 1) * 128)
             send_ref[2 * hh, :, cols] = jnp.where(lo64, a, swap(b)).astype(BF)
             send_ref[2 * hh + 1, :, cols] = jnp.where(lo64, swap(a), b).astype(BF)
+    grads_ref[:, :1536] = outer(second_ref[...], d_qkv_ref[...])
+    grads_ref[:, 1536:2048] = outer(heads_one_ref[...], d_middle)
+    grads_ref[:, 2048:] = outer(heads_two_ref[...], up_ref[...])
+    core = core_ref[0]
+    keep_ref[...] = grads_ref[:, pl.ds(pl.multiple_of(core * 1280, 1280), 1280)]
+    give_ref[...] = grads_ref[:, pl.ds(pl.multiple_of((1 - core) * 1280, 1280), 1280)]
 
 
 def last_kernel(got_ref, w_ref, tokens_ref, gain_ref, d_middle_ref, out_ref, d_qkv_ref):
@@ -294,33 +307,31 @@
     out_ref[:, 128:192] = sums[2][:, :HD].astype(BF)
 
 
-def call(kernel, outs, args, scratch=(), flops=10**9, moved=4 * 10**6, exps=0):
+def call(kernel, outs, args, scratch=(), flops=10**9, moved=4 * 10**6, exps=0, vmem=LARGE):
     return pl.pallas_call(
         kernel,
         out_shape=[jax.ShapeDtypeStruct(shape, dtype) for shape, dtype in outs],
         scratch_shapes=list(scratch),
-        compiler_params=pltpu.CompilerParams(vmem_limit_bytes=VMEM_LIMIT),
+        in_specs=[
+            pl.BlockSpec(memory_space=pltpu.SMEM if x.dtype == jnp.int32 else pltpu.VMEM) for x in args
+        ],
+        compiler_params=pltpu.CompilerParams(vmem_limit_bytes=vmem),
         cost_estimate=pl.CostEstimate(flops=flops, bytes_accessed=moved, transcendentals=exps),
     )(*args)
 
 
-def outer(left, right):
-    return lax.dot_general(
-        left, right, (((0,), (0,)), ((), ())), preferred_element_type=F32
-    ).astype(BF)
-
-
 def to_markers(x):
     lead = x.shape[:-2]
-    k = len(lead)
-    x = x.reshape(*lead, 6, 8, 8, 512)
-    order = (k + 1, *range(k), k, k + 2, k + 3)
-    x = jnp.transpose(x, order)
-    x = lax.all_to_all(x, "marker", 0, 0, tiled=True)
-    back = [0] * len(order)
-    for i, o in enumerate(order):
-        back[o] = i
-    return jnp.transpose(x, back).reshape(*lead, 384, 512)
+    k = len(lead) + 1
+    n = lax.axis_size("marker")
+    me = lax.axis_index("marker")
+    x = x.reshape(*lead, 6, n, 8, 512)
+    out = x
+    for step in (4, 3, 5, 2, 6, 1, 7):
+        give = lax.dynamic_slice_in_dim(x, lax.rem(me + step, n), 1, k)
+        got = lax.ppermute(give, "marker", [(i, (i + step) % n) for i in range(n)])
+        out = lax.dynamic_update_slice_in_dim(out, got, lax.rem(me + n - step, n), k)
+    return out.reshape(*lead, 384, 512)
 
 
 def swapped(x, bit):
@@ -328,11 +339,16 @@
     return lax.ppermute(x, "batch", [(i, i ^ bit) for i in range(n)])
 
 
-def halve(x, bit, shift):
+def halves(x, shift):
     width = x.shape[1] // 2
     mine = (lax.axis_index("batch") >> shift) & 1
     keep = lax.dynamic_slice_in_dim(x, mine * width, width, 1)
     give = lax.dynamic_slice_in_dim(x, (1 - mine) * width, width, 1)
+    return keep, give
+
+
+def halve(x, bit, shift):
+    keep, give = halves(x, shift)
     return (keep.astype(F32) + swapped(give, bit).astype(F32)).astype(BF)
 
 
@@ -346,58 +362,66 @@
     gain_1 = gain_first.reshape(1, 512)
     gain_2 = gain_second.reshape(1, 512)
 
-    first, qkv_send = call(
+    first_t, qkv_send = call(
         project_kernel,
-        [((384, 512), BF), ((8, 64, 1152), BF)],
+        [((512, 384), BF), ((8, 64, 1152), BF)],
         (mine, gain_1, w_qkv_space),
     )
     qkv_one = lax.all_to_all(qkv_send, "space", 0, 0, tiled=True).reshape(512, 1152)
     wide = to_markers(jnp.stack([mine, up_mine]))
-    first_all = lax.all_gather(first.T, "space", axis=0, tiled=False)
+    first_all = lax.all_gather(first_t, "space", axis=0, tiled=False)
 
     heads, inv = call(
         spatial_kernel, [((512, 384), BF), ((6, 512), F32)], (qkv_one,),
-        flops=2 * 10**9, exps=6 * 512 * 512,
+        flops=2 * 10**9, exps=6 * 512 * 512, vmem=SMALL,
     )
     got = lax.all_to_all(heads, both, 0, 0, tiled=True).reshape(8, 64, 384)
 
     up_all = wide[1]
-    heads_one, second, d_qkv_two, heads_two, d_middle, d_send = call(
+    core = (lax.axis_index("batch") & 1).astype(jnp.int32).reshape(1)
+    keep, give, d_middle, d_send = call(
         middle_kernel,
-        [((384, 512), BF), ((384, 512), BF), ((384, 1536), BF), ((384, 512), BF),
-         ((384, 512), BF), ((8, 64, 384), BF)],
-        (got, wide[0], up_all, w_out_space, gain_2, w_qkv_marker, w_out_marker),
-        scratch=[pltpu.VMEM((384, 1536), BF), pltpu.VMEM((384, 512), BF)],
-        flops=6 * 10**9, exps=8 * 384 * 384,
+        [((512, 1280), BF), ((512, 1280), BF), ((384, 512), BF), ((8, 64, 384), BF)],
+        (core, got, wide[0], up_all, w_out_space, gain_2, w_qkv_marker, w_out_marker),
+        scratch=[
+            pltpu.VMEM(shape, BF)
+            for shape in ((512, 2560), (384, 512), (384, 512), (384, 1536), (384, 512), (384, 1536), (384, 512))
+        ],
+        flops=6 * 10**9, exps=8 * 384 * 384, vmem=LARGE,
     )
     d_heads = lax.all_to_all(d_send.reshape(512, 384), both, 0, 0, tiled=True)
-    d_middle_mine = to_markers(d_middle)
-
+
+    d_heads, first_all = lax.optimization_barrier((d_heads, first_all))
     d_qkv_one, = call(
         spatial_back_kernel, [((512, 1152), BF)], (qkv_one, heads, inv, d_heads),
-        flops=5 * 10**9, exps=6 * 512 * 512,
-    )
+        flops=10**6, moved=10**4, vmem=SMALL,
+    )
+    middle_all = lax.all_gather(d_middle, "marker", axis=0, tiled=False)
+    share, give = halves((keep.astype(F32) + swapped(give, 1).astype(F32)).astype(BF), 1)
+    give = swapped(give, 2)
+    d_qkv_one, give = lax.optimization_barrier((d_qkv_one, give))
     d_back = lax.all_to_all(d_qkv_one, "space", 0, 0, tiled=True).reshape(8, 64, 1152)
+    first_all, middle_all = lax.optimization_barrier((first_all, middle_all))
+    share = (share.astype(F32) + give.astype(F32)).astype(BF)
+    column, = call(column_kernel, [((512, 192), BF)], (first_all, d_qkv_one), flops=2 * 10**9)
+    shares = jnp.concatenate([share, column], axis=1)
+    shares, d_back = lax.optimization_barrier((shares, d_back))
+    d_middle_mine = lax.dynamic_index_in_dim(
+        middle_all.reshape(8, 6, 8, 8, 512), lax.axis_index("marker"), 2, keepdims=False
+    )
+    d_middle_mine = jnp.transpose(d_middle_mine, (1, 0, 2, 3)).reshape(384, 512)
+    shares = lax.all_to_all(shares, rows, 0, 0, tiled=True).reshape(8, 8, 8, 832).astype(F32)
+    column = jnp.sum(shares[..., 640:], axis=0).transpose(1, 0, 2).reshape(8, 1536)
+    share = jnp.sum(shares[..., :640], axis=(0, 1))
+    share = jnp.concatenate([share, column], axis=1).astype(BF)
+    share = lax.all_gather(share, "batch", axis=0, tiled=False)
+    share = share.reshape(2, 2, 8, 2176).astype(F32)
+    column = jnp.sum(share[..., 640:], axis=(0, 1))
+    share = share[..., :640].transpose(2, 1, 0, 3).reshape(8, 2560)
     d_tokens, = call(
         last_kernel, [((384, 512), BF)], (d_back, w_qkv_space, mine, gain_1, d_middle_mine),
-        scratch=[pltpu.VMEM((384, 1536), BF)],
-    )
-
-    grads = jnp.concatenate(
-        [outer(second, d_qkv_two), outer(heads_one, d_middle), outer(heads_two, up_all)], axis=1
-    )
-    share = halve(halve(grads, 1, 0), 2, 1)
-    share = lax.all_to_all(share, rows, 0, 0, tiled=True)
-    share = jnp.sum(share.reshape(64, 8, 640).astype(F32), axis=0).astype(BF)
-    share = lax.all_gather(share, "batch", axis=0, tiled=False)
-    share = share.reshape(2, 2, 8, 640).transpose(2, 1, 0, 3).reshape(8, 2560).astype(F32)
-
-    column, = call(column_kernel, [((512, 192), BF)], (first_all, d_qkv_one), flops=2 * 10**9)
-    column = lax.all_to_all(column, rows, 0, 0, tiled=True)
-    column = jnp.sum(column.reshape(8, 8, 8, 192).astype(F32), axis=0)
-    column = column.transpose(1, 0, 2).reshape(8, 1536).astype(BF)
-    column = lax.all_gather(column, "batch", axis=0, tiled=False)
-    column = jnp.sum(column.astype(F32), axis=0)
+        scratch=[pltpu.VMEM((384, 1536), BF)], vmem=SMALL,
+    )
 
     count = 1
     for axis in ("batch", "marker", "space"):
@@ -405,9 +429,11 @@
     factor = 1.0 / math.sqrt(count * 384)
     at = (lax.axis_index("marker") * 8 + lax.axis_index("space")) * 8
 
+    own = [lax.dynamic_slice_in_dim(x, at, 8, 0) for x in (w_qkv_space, gain_first, w_qkv_marker, gain_second)]
+    own = lax.optimization_barrier(own)
+
     def gain_grad(weight, gain, grad):
-        w = lax.dynamic_slice_in_dim(weight, at, 8, 0).astype(F32)
-        return jnp.sum(w * grad, axis=1) / lax.dynamic_slice_in_dim(gain, at, 8, 0)
+        return jnp.sum(weight.astype(F32) * grad, axis=1) / gain
 
     g_qkv_space = column * factor
     g_qkv_marker = share[:, :1536] * factor
@@ -415,10 +441,10 @@
         jnp.transpose(d_tokens.reshape(6, 64, 512), (1, 0, 2))[None],
         g_qkv_space,
         share[:, 1536:2048] * factor,
-        gain_grad(w_qkv_space, gain_first, g_qkv_space),
+        gain_grad(own[0], own[1], g_qkv_space),
         g_qkv_marker,
         share[:, 2048:] * factor,
-        gain_grad(w_qkv_marker, gain_second, g_qkv_marker),
+        gain_grad(own[2], own[3], g_qkv_marker),
     )
 
 

time: 268 us -> 197 us (0.74)
  waiting for transfers between devices: 115 us -> 57 us
  blocking collectives: 17 us -> 9.26 us
  matrix products: 4.38 us -> 0 us
  starting transfers between devices: 55.8 us -> 59 us
    ppermute x2, waiting for transfers between devices: 24.5 us -> 0.01 us  [swapped(): return lax.ppermute(x, 'batch', [(i, i ^ bit) for i in range(n)])]
    all_to_all x4 -> x1, waiting for transfers between devices: 43.4 us -> 19 us  [on_device(): lax.all_to_all(shares, rows, 0, 0, tiled=True).reshape(8, 8, 8, 832)]
    all_to_all x4 -> x1, starting transfers between devices: 31.7 us -> 9.89 us  [on_device(): lax.all_to_all(shares, rows, 0, 0, tiled=True).reshape(8, 8, 8, 832)]
    all_to_all x1, waiting for transfers between devices: 17.6 us -> 0.8 us  [on_device(): lax.all_to_all(qkv_send, 'space', 0, 0, tiled=True).reshape(512, 1152)]
    ppermute x0 -> x7, starting transfers between devices: none -> 15.8 us  [to_markers(): got = lax.ppermute(give, 'marker', [(i, (i + step) % n) for i in range(n)])]
    all_gather x1 -> x2, waiting for transfers between devices: 0.01 us -> 10.8 us  [the longest x1 10.8 us: on_device(): middle_all = lax.all_gather(d_middle, 'marker', axis=0, tiled=False)]
    all_gather x1 -> x0, blocking collectives: 7.36 us -> none  [on_device(): column = lax.all_gather(column, 'batch', axis=0, tiled=False)]
    all_to_all x1, starting transfers between devices: 4.63 us -> 11 us  [on_device(): got = lax.all_to_all(heads, both, 0, 0, tiled=True).reshape(8, 64, 384)]
  transfers between devices with their start and end apart: 11 -> 16, of which waited for: 8 -> 6; matrix products, arithmetic and copies ran while one was open for 7% -> 7% of each run, Pallas kernels for 11% -> 17%
where the time goes in v2:
time: 197 us; the launch traced here: 196 us
  starting transfers between devices  59 us (30%)
  waiting for transfers between devices  57 us (29%)
  Pallas kernels  36.4 us (18%)
  between operations  14.3 us (7%)
  other arithmetic  11 us (6%)
  local copies, waits for them, and re-layouts  9.42 us (5%)
  blocking collectives  9.26 us (5%)
    pallas_call x6, Pallas kernels, call(): pl.pallas_call(kernel, out_shape=[jax.ShapeDtypeStruct(shape, dtype) for...  36.4 us
    all_to_all x1, waiting for transfers between devices, on_device(): lax.all_to_all(shares, rows, 0, 0, tiled=True).reshape(8, 8, 8, 832)  19 us
    ppermute x7, starting transfers between devices, to_markers(): got = lax.ppermute(give, 'marker', [(i, (i + step) % n) for i in range(n)])  15.8 us
    all_to_all x1, waiting for transfers between devices, on_device(): d_heads = lax.all_to_all(d_send.reshape(512, 384), both, 0, 0, tiled=True)  11.9 us
    all_to_all x1, starting transfers between devices, on_device(): got = lax.all_to_all(heads, both, 0, 0, tiled=True).reshape(8, 64, 384)  11 us
    all_gather x1, waiting for transfers between devices, on_device(): middle_all = lax.all_gather(d_middle, 'marker', axis=0, tiled=False)  10.8 us
    all_to_all x1, waiting for transfers between devices, on_device(): got = lax.all_to_all(heads, both, 0, 0, tiled=True).reshape(8, 64, 384)  10.5 us
    all_to_all x1, starting transfers between devices, on_device(): lax.all_to_all(shares, rows, 0, 0, tiled=True).reshape(8, 8, 8, 832)  9.89 us
  transfers between devices with their start and end apart: 16, of which 6 were waited for; matrix products, arithmetic and copies ran while one was open for 7% of the time, Pallas kernels for 17%

profile of v2, /device:TPU:1, one launch (start us, length us, event | category | flops | bytes accessed | tf_op | source)
XLA Modules:
  0.0 196.2 jit_solution(9866756553856112382)
XLA Ops:
  7.2 3.7 %shard_map.135 = (bf16[512,384]{1,0:T(8,128)(2,1)}, bf16[8,64,1152]{2,1,0:T(8,128)(2,1)}) custom-call(bf16[384,512]{1,0:T(8,128)(2,1)} %bitcast.51, f32[1,512]{1,0:T(1,128)} %bitcast.60, bf16[512,1536]{1,0:T(8,128)(2,1)} %w_ref.3), custom_call_target="tpu_custom_call" | custom-call | flops 1000000000 | bytes 4000000 | tf_op jit(solution)/shard_map/pallas_call | solution.py:311
  11.0 7.6 %all-to-all-start = ((bf16[8,64,1152]{2,1,0:T(8,128)(2,1)}), bf16[8,64,1152]{2,1,0:T(8,128)(2,1)S(1)}, u32[]{:S(2)}, u32[]{:S(2)}) async-start(bf16[8,64,1152]{2,1,0:T(8,128)(2,1)} %get-tuple-element.27), calls=%async_computation | async-start | bytes 2359296 | tf_op jit(solution)/shard_map/all_to_all | solution.py:370
  18.7 7.0 %collective-permute-start = (bf16[2,6,1,8,512]{4,3,2,1,0:T(8,128)(2,1)S(1)}, bf16[2,6,1,8,512]{4,3,2,1,0:T(8,128)(2,1)S(1)}, u32[]{:S(2)}, u32[]{:S(2)}) collective-permute-start(bf16[2,6,1,8,512]{4,3,2,1,0:T(8,128)(2,1)S(1)} %get-tuple-element.54), channel_id=1, source_target_pairs={{0,32},{8,40},{16,48},{24,56},{32,0},{40,8},{48,16},{56,24},{1,33}... | collective-permute-start | bytes 294920 | tf_op jit(solution)/shard_map/ppermute | solution.py:332
  27.3 2.8 %collective-permute-start.2 = (bf16[2,6,1,8,512]{4,3,2,1,0:T(8,128)(2,1)S(1)}, bf16[2,6,1,8,512]{4,3,2,1,0:T(8,128)(2,1)}, u32[]{:S(2)}, u32[]{:S(2)}) collective-permute-start(bf16[2,6,1,8,512]{4,3,2,1,0:T(8,128)(2,1)S(1)} %get-tuple-element.56), channel_id=1, source_target_pairs={{0,40},{8,48},{16,56},{24,0},{32,8},{40,16},{48,24},{56,32},{1,41}... | collective-permute-start | bytes 294920 | tf_op jit(solution)/shard_map/ppermute | solution.py:332
  31.3 2.4 %collective-permute-start.4 = (bf16[2,6,1,8,512]{4,3,2,1,0:T(8,128)(2,1)S(1)}, bf16[2,6,1,8,512]{4,3,2,1,0:T(8,128)(2,1)}, u32[]{:S(2)}, u32[]{:S(2)}) collective-permute-start(bf16[2,6,1,8,512]{4,3,2,1,0:T(8,128)(2,1)S(1)} %get-tuple-element.58), channel_id=1, source_target_pairs={{0,48},{8,56},{16,0},{24,8},{32,16},{40,24},{48,32},{56,40},{1,49}... | collective-permute-start | bytes 294920 | tf_op jit(solution)/shard_map/ppermute | solution.py:332
  35.2 3.9 %collective-permute-done.1 = bf16[2,6,1,8,512]{4,3,2,1,0:T(8,128)(2,1)S(1)} collective-permute-done((bf16[2,6,1,8,512]{4,3,2,1,0:T(8,128)(2,1)S(1)}, bf16[2,6,1,8,512]{4,3,2,1,0:T(8,128)(2,1)S(1)}, u32[]{:S(2)}, u32[]{:S(2)}) %collective-permute-start.1) | collective-permute-done | bytes 98336 | tf_op jit(solution)/shard_map/ppermute | solution.py:332
  39.9 4.5 %shard_map.136 = (bf16[512,384]{1,0:T(8,128)(2,1)}, f32[6,512]{1,0:T(8,128)S(1)}) custom-call(bf16[512,1152]{1,0:T(8,128)(2,1)S(1)} %bitcast.56), custom_call_target="tpu_custom_call" | custom-call | flops 2000000000 | bytes 4000000 | tf_op jit(solution)/shard_map/pallas_call | solution.py:311
  44.4 11.0 %all-to-all-start.1 = ((bf16[64,8,384]{2,1,0:T(8,128)(2,1)}), bf16[64,8,384]{2,1,0:T(8,128)(2,1)S(1)}, u32[]{:S(2)}, u32[]{:S(2)}) async-start(bf16[64,8,384]{2,1,0:T(8,128)(2,1)} %bitcast.6), calls=%async_computation.1 | async-start | bytes 786432 | tf_op jit(solution)/shard_map/all_to_all | solution.py:378
  59.5 10.5 %all-to-all-done.1 = bf16[64,8,384]{2,1,0:T(8,128)(2,1)S(1)} async-done(((bf16[64,8,384]{2,1,0:T(8,128)(2,1)}), bf16[64,8,384]{2,1,0:T(8,128)(2,1)S(1)}, u32[]{:S(2)}, u32[]{:S(2)}) %all-to-all-start.1) | async-done | bytes 393248 | tf_op jit(solution)/shard_map/all_to_all | solution.py:378
  70.7 13.4 %shard_map.137 = (bf16[512,1280]{1,0:T(8,128)(2,1)}, bf16[512,1280]{1,0:T(8,128)(2,1)}, bf16[384,512]{1,0:T(8,128)(2,1)}, bf16[8,64,384]{2,1,0:T(8,128)(2,1)}) custom-call(s32[1]{0:T(128)} %bitcast.core_ref, bf16[8,64,384]{2,1,0:T(8,128)(2,1)} %bitcast.67, bf16[384,512]{1,0:T(8,128)(2,1)} %bitcast.70, bf16[384,512]{1,0:T(8,128)(2,1)} %bitcast.69, ...), custom_call_target="tpu_custom_call" | custom-call | flops 6000000000 | bytes 4000000 | tf_op jit(solution)/shard_map/pallas_call | solution.py:311
  84.2 4.2 %collective-permute-start.7 = (bf16[512,1280]{1,0:T(8,128)(2,1)}, bf16[512,1280]{1,0:T(8,128)(2,1)S(1)}, u32[]{:S(2)}, u32[]{:S(2)}) collective-permute-start(bf16[512,1280]{1,0:T(8,128)(2,1)} %get-tuple-element.30), channel_id=1, source_target_pairs={{0,64},{64,0},{128,192},{192,128},{1,65},{65,1},{129,193},{193,129... | collective-permute-start | bytes 3932168 | tf_op jit(solution)/shard_map/ppermute | solution.py:339
  88.3 4.6 %all-to-all-start.2 = ((bf16[64,8,384]{2,1,0:T(8,128)(2,1)}), bf16[64,8,384]{2,1,0:T(8,128)(2,1)S(1)}, u32[]{:S(2)}, u32[]{:S(2)}) async-start(bf16[64,8,384]{2,1,0:T(8,128)(2,1)} %bitcast.68), calls=%async_computation.2 | async-start | bytes 786432 | tf_op jit(solution)/shard_map/all_to_all | solution.py:392
  94.1 2.0 %add_convert_fusion = bf16[512,1280]{1,0:T(8,128)(2,1)S(1)} fusion(bf16[512,1280]{1,0:T(8,128)(2,1)} %copy-done.5, bf16[512,1280]{1,0:T(8,128)(2,1)} %get-tuple-element.29), kind=kLoop, calls=%fused_computation | loop fusion | flops 2621440 | bytes 3932160 | tf_op jit(solution)/shard_map/convert_element_type | solution.py:400
  97.3 11.9 %all-to-all-done.2 = bf16[64,8,384]{2,1,0:T(8,128)(2,1)S(1)} async-done(((bf16[64,8,384]{2,1,0:T(8,128)(2,1)}), bf16[64,8,384]{2,1,0:T(8,128)(2,1)S(1)}, u32[]{:S(2)}, u32[]{:S(2)}) %all-to-all-start.2) | async-done | bytes 393248 | tf_op jit(solution)/shard_map/all_to_all | solution.py:392
  109.2 7.7 %shard_map.138.d_qkv_ref = bf16[512,1152]{1,0:T(8,128)(2,1)} custom-call(bf16[512,1152]{1,0:T(8,128)(2,1)S(1)} %bitcast.57, bf16[512,384]{1,0:T(8,128)(2,1)} %get-tuple-element.28.heads_ref, f32[6,512]{1,0:T(8,128)S(1)} %get-tuple-element.31.inv_ref, bf16[512,384]{1,0:T(8,128)(2,1)S(1)} %bitcast.58), custom_call_target="tpu_custom_call" | custom-call | flops 1000000 | bytes 10000 | tf_op jit(solution)/shard_map/pallas_call | solution.py:311
  116.9 5.4 %all-to-all-start.3 = ((bf16[8,64,1152]{2,1,0:T(8,128)(2,1)}), bf16[8,64,1152]{2,1,0:T(8,128)(2,1)S(1)}, u32[]{:S(2)}, u32[]{:S(2)}) async-start(bf16[8,64,1152]{2,1,0:T(8,128)(2,1)} %bitcast.20), calls=%async_computation.3 | async-start | bytes 2359296 | tf_op jit(solution)/shard_map/all_to_all | solution.py:403
  122.3 2.1 %add_convert_fusion.1 = bf16[512,640]{1,0:T(8,128)(2,1)} fusion(bf16[512,640]{1,0:T(8,128)(2,1)} %collective-permute-done.8, bf16[512,1280]{1,0:T(8,128)(2,1)S(1)} %add_convert_fusion, s32[]{:T(128)S(6)} %select_n.51), kind=kLoop, calls=%fused_computation.17 | loop fusion | flops 1310720 | bytes 1966084 | tf_op jit(solution)/shard_map/convert_element_type | solution.py:405
  124.4 10.8 %all-gather.7.cloned.1.call-done = bf16[3072,512]{1,0:T(8,128)(2,1)} async-done(((bf16[384,512]{1,0:T(8,128)(2,1)}), bf16[3072,512]{1,0:T(8,128)(2,1)}) %all-gather.7.cloned.1.call-update) | async-done | bytes 3145744 | tf_op jit(solution)/shard_map/all_gather | solution.py:399
  135.2 5.2 %shard_map.139 = bf16[512,192]{1,0:T(8,128)(2,1)} custom-call(bf16[8,512,384]{2,1,0:T(8,128)(2,1)} %bitcast.74, bf16[512,1152]{1,0:T(8,128)(2,1)} %shard_map.138.d_qkv_ref), custom_call_target="tpu_custom_call" | custom-call | flops 2000000000 | bytes 4000000 | tf_op jit(solution)/shard_map/pallas_call | solution.py:311
  140.4 2.1 %pad_maximum_fusion.1 = bf16[512,832]{1,0:T(8,128)(2,1)} fusion(bf16[512,192]{1,0:T(8,128)(2,1)} %shard_map.139, bf16[512,640]{1,0:T(8,128)(2,1)S(1)} %copy-done.4), kind=kLoop, calls=%fused_computation.18 | loop fusion | flops 1703936 | bytes 1703936 | tf_op jit(solution)/shard_map/concatenate | solution.py:407
  142.5 9.9 %all-to-all-start.4 = ((bf16[64,8,832]{2,1,0:T(8,128)(2,1)}), bf16[64,8,832]{2,1,0:T(8,128)(2,1)}, u32[]{:S(2)}, u32[]{:S(2)}) async-start(bf16[64,8,832]{2,1,0:T(8,128)(2,1)} %bitcast.62), calls=%async_computation.4 | async-start | bytes 1835008 | tf_op jit(solution)/shard_map/all_to_all | solution.py:413
  155.1 1.8 shard_map.140
  156.9 19.0 %all-to-all-done.4 = bf16[64,8,832]{2,1,0:T(8,128)(2,1)} async-done(((bf16[64,8,832]{2,1,0:T(8,128)(2,1)}), bf16[64,8,832]{2,1,0:T(8,128)(2,1)}, u32[]{:S(2)}, u32[]{:S(2)}) %all-to-all-start.4) | async-done | bytes 852000 | tf_op jit(solution)/shard_map/all_to_all | solution.py:413
  177.5 9.3 %all_gather.20 = bf16[4,8,2176]{2,1,0:T(8,128)(2,1)S(1)} all-gather(bf16[1,8,2176]{2,1,0:T(8,128)(2,1)S(1)} %pad_maximum_fusion.2), channel_id=1, replica_groups=mesh['batch'=4,'marker'=8,'space'=8] {'batch'}, dimensions={0}, use_global_device_ids=true | all-gather | bytes 174080 | tf_op jit(solution)/shard_map/all_gather | solution.py:417
  (67 shorter events, 19.1 us)
Async XLA Ops:
  7.2 102.0 %all-gather.5.cloned.1.call-start = ((), (), s32[]{:S(2)}) async-start(), calls=%async_computation.5 | async-start | bytes 3538944 | tf_op jit(solution)/shard_map/all_gather | solution.py:372
  10.9 7.6 %copy-start = (bf16[1,64,6,512]{3,1,2,0:T(8,128)(2,1)S(1)}, bf16[1,64,6,512]{3,1,2,0:T(8,128)(2,1)}, u32[]{:S(2)}) copy-start(bf16[1,64,6,512]{3,1,2,0:T(8,128)(2,1)} %param.8) | copy-start | bytes 1179652
  10.9 7.6 %copy-start.3 = (bf16[1,64,6,512]{3,1,2,0:T(8,128)(2,1)S(1)}, bf16[1,64,6,512]{3,1,2,0:T(8,128)(2,1)}, u32[]{:S(2)}) copy-start(bf16[1,64,6,512]{3,1,2,0:T(8,128)(2,1)} %param.15) | copy-start | bytes 1179652
  11.0 29.0 %all-to-all-start = ((bf16[8,64,1152]{2,1,0:T(8,128)(2,1)}), bf16[8,64,1152]{2,1,0:T(8,128)(2,1)S(1)}, u32[]{:S(2)}, u32[]{:S(2)}) async-start(bf16[8,64,1152]{2,1,0:T(8,128)(2,1)} %get-tuple-element.27), calls=%async_computation | async-start | bytes 2359296 | tf_op jit(solution)/shard_map/all_to_all | solution.py:370
  18.7 15.8 %collective-permute-start = (bf16[2,6,1,8,512]{4,3,2,1,0:T(8,128)(2,1)S(1)}, bf16[2,6,1,8,512]{4,3,2,1,0:T(8,128)(2,1)S(1)}, u32[]{:S(2)}, u32[]{:S(2)}) collective-permute-start(bf16[2,6,1,8,512]{4,3,2,1,0:T(8,128)(2,1)S(1)} %get-tuple-element.54), channel_id=1, source_target_pairs={{0,32},{8,40},{16,48},{24,56},{32,0},{40,8},{48,16},{56,24},{1,33}... | collective-permute-start | bytes 294920 | tf_op jit(solution)/shard_map/ppermute | solution.py:332
  25.7 13.4 %collective-permute-start.1 = (bf16[2,6,1,8,512]{4,3,2,1,0:T(8,128)(2,1)S(1)}, bf16[2,6,1,8,512]{4,3,2,1,0:T(8,128)(2,1)S(1)}, u32[]{:S(2)}, u32[]{:S(2)}) collective-permute-start(bf16[2,6,1,8,512]{4,3,2,1,0:T(8,128)(2,1)S(1)} %get-tuple-element.55), channel_id=1, source_target_pairs={{0,24},{8,32},{16,40},{24,48},{32,56},{40,0},{48,8},{56,16},{1,25}... | collective-permute-start | bytes 294920 | tf_op jit(solution)/shard_map/ppermute | solution.py:332
  27.3 28.4 %collective-permute-start.2 = (bf16[2,6,1,8,512]{4,3,2,1,0:T(8,128)(2,1)S(1)}, bf16[2,6,1,8,512]{4,3,2,1,0:T(8,128)(2,1)}, u32[]{:S(2)}, u32[]{:S(2)}) collective-permute-start(bf16[2,6,1,8,512]{4,3,2,1,0:T(8,128)(2,1)S(1)} %get-tuple-element.56), channel_id=1, source_target_pairs={{0,40},{8,48},{16,56},{24,0},{32,8},{40,16},{48,24},{56,32},{1,41}... | collective-permute-start | bytes 294920 | tf_op jit(solution)/shard_map/ppermute | solution.py:332
  30.1 26.5 %collective-permute-start.3 = (bf16[2,6,1,8,512]{4,3,2,1,0:T(8,128)(2,1)S(1)}, bf16[2,6,1,8,512]{4,3,2,1,0:T(8,128)(2,1)}, u32[]{:S(2)}, u32[]{:S(2)}) collective-permute-start(bf16[2,6,1,8,512]{4,3,2,1,0:T(8,128)(2,1)S(1)} %get-tuple-element.57), channel_id=1, source_target_pairs={{0,16},{8,24},{16,32},{24,40},{32,48},{40,56},{48,0},{56,8},{1,17}... | collective-permute-start | bytes 294920 | tf_op jit(solution)/shard_map/ppermute | solution.py:332
  31.3 26.2 %collective-permute-start.4 = (bf16[2,6,1,8,512]{4,3,2,1,0:T(8,128)(2,1)S(1)}, bf16[2,6,1,8,512]{4,3,2,1,0:T(8,128)(2,1)}, u32[]{:S(2)}, u32[]{:S(2)}) collective-permute-start(bf16[2,6,1,8,512]{4,3,2,1,0:T(8,128)(2,1)S(1)} %get-tuple-element.58), channel_id=1, source_target_pairs={{0,48},{8,56},{16,0},{24,8},{32,16},{40,24},{48,32},{56,40},{1,49}... | collective-permute-start | bytes 294920 | tf_op jit(solution)/shard_map/ppermute | solution.py:332
  34.5 24.0 %collective-permute-start.5 = (bf16[2,6,1,8,512]{4,3,2,1,0:T(8,128)(2,1)}, bf16[2,6,1,8,512]{4,3,2,1,0:T(8,128)(2,1)S(1)}, u32[]{:S(2)}, u32[]{:S(2)}) collective-permute-start(bf16[2,6,1,8,512]{4,3,2,1,0:T(8,128)(2,1)} %fusion.5), channel_id=1, source_target_pairs={{0,8},{8,16},{16,24},{24,32},{32,40},{40,48},{48,56},{56,0},{1,9},... | collective-permute-start | bytes 294920 | tf_op jit(solution)/shard_map/ppermute | solution.py:332
  39.1 19.4 %collective-permute-start.6 = (bf16[2,6,1,8,512]{4,3,2,1,0:T(8,128)(2,1)S(1)}, bf16[2,6,1,8,512]{4,3,2,1,0:T(8,128)(2,1)S(1)}, u32[]{:S(2)}, u32[]{:S(2)}) collective-permute-start(bf16[2,6,1,8,512]{4,3,2,1,0:T(8,128)(2,1)S(1)} %get-tuple-element.53), channel_id=1, source_target_pairs={{0,56},{8,0},{16,8},{24,16},{32,24},{40,32},{48,40},{56,48},{1,57}... | collective-permute-start | bytes 294920 | tf_op jit(solution)/shard_map/ppermute | solution.py:332
  44.4 25.5 %all-to-all-start.1 = ((bf16[64,8,384]{2,1,0:T(8,128)(2,1)}), bf16[64,8,384]{2,1,0:T(8,128)(2,1)S(1)}, u32[]{:S(2)}, u32[]{:S(2)}) async-start(bf16[64,8,384]{2,1,0:T(8,128)(2,1)} %bitcast.6), calls=%async_computation.1 | async-start | bytes 786432 | tf_op jit(solution)/shard_map/all_to_all | solution.py:378
  55.5 79.8 %all-gather.7.cloned.1.call-start = ((), (), s32[]{:S(2)}) async-start(), calls=%async_computation.6 | async-start | bytes 3538944 | tf_op jit(solution)/shard_map/all_gather | solution.py:399
  70.0 0.7 copy-start.6
  84.2 8.8 %collective-permute-start.7 = (bf16[512,1280]{1,0:T(8,128)(2,1)}, bf16[512,1280]{1,0:T(8,128)(2,1)S(1)}, u32[]{:S(2)}, u32[]{:S(2)}) collective-permute-start(bf16[512,1280]{1,0:T(8,128)(2,1)} %get-tuple-element.30), channel_id=1, source_target_pairs={{0,64},{64,0},{128,192},{192,128},{1,65},{65,1},{129,193},{193,129... | collective-permute-start | bytes 3932168 | tf_op jit(solution)/shard_map/ppermute | solution.py:339
  88.3 20.8 %all-to-all-start.2 = ((bf16[64,8,384]{2,1,0:T(8,128)(2,1)}), bf16[64,8,384]{2,1,0:T(8,128)(2,1)S(1)}, u32[]{:S(2)}, u32[]{:S(2)}) async-start(bf16[64,8,384]{2,1,0:T(8,128)(2,1)} %bitcast.68), calls=%async_computation.2 | async-start | bytes 786432 | tf_op jit(solution)/shard_map/all_to_all | solution.py:392
  93.0 1.1 copy-start.5
  97.1 19.8 %collective-permute-start.8 = (bf16[512,640]{1,0:T(8,128)(2,1)}, bf16[512,640]{1,0:T(8,128)(2,1)}, u32[]{:S(2)}, u32[]{:S(2)}) collective-permute-start(bf16[512,640]{1,0:T(8,128)(2,1)} %constant_dynamic-slice_fusion.3), channel_id=1, source_target_pairs={{0,128},{64,192},{128,0},{192,64},{1,129},{65,193},{129,1},{193,65... | collective-permute-start | bytes 1966088 | tf_op jit(solution)/shard_map/ppermute | solution.py:339
  116.9 25.6 %all-to-all-start.3 = ((bf16[8,64,1152]{2,1,0:T(8,128)(2,1)}), bf16[8,64,1152]{2,1,0:T(8,128)(2,1)S(1)}, u32[]{:S(2)}, u32[]{:S(2)}) async-start(bf16[8,64,1152]{2,1,0:T(8,128)(2,1)} %bitcast.20), calls=%async_computation.3 | async-start | bytes 2359296 | tf_op jit(solution)/shard_map/all_to_all | solution.py:403
  135.2 5.2 %copy-start.4 = (bf16[512,640]{1,0:T(8,128)(2,1)S(1)}, bf16[512,640]{1,0:T(8,128)(2,1)}, u32[]{:S(2)}) copy-start(bf16[512,640]{1,0:T(8,128)(2,1)} %add_convert_fusion.1) | copy-start | bytes 1966084
  140.4 12.0 %copy-start.2 = (f32[512]{0:T(512)S(1)}, f32[512]{0:T(512)}, u32[]{:S(2)}) copy-start(f32[512]{0:T(512)} %param.9) | copy-start | bytes 6148
  140.4 13.6 %copy-start.1 = (bf16[512,1536]{1,0:T(8,128)(2,1)S(1)}, bf16[512,1536]{1,0:T(8,128)(2,1)}, u32[]{:S(2)}) copy-start(bf16[512,1536]{1,0:T(8,128)(2,1)} %w_ref.3) | copy-start | bytes 4718596
  142.5 33.4 %all-to-all-start.4 = ((bf16[64,8,832]{2,1,0:T(8,128)(2,1)}), bf16[64,8,832]{2,1,0:T(8,128)(2,1)}, u32[]{:S(2)}, u32[]{:S(2)}) async-start(bf16[64,8,832]{2,1,0:T(8,128)(2,1)} %bitcast.62), calls=%async_computation.4 | async-start | bytes 1835008 | tf_op jit(solution)/shard_map/all_to_all | solution.py:413
Sparse Core Ops, SparseCore 0:
  11.2 79.3 all-gather.4
  92.4 42.8 all-gather.6

commit v3 on v2

--- a/solution.py
+++ b/solution.py
@@ -401,22 +401,23 @@
     give = swapped(give, 2)
     d_qkv_one, give = lax.optimization_barrier((d_qkv_one, give))
     d_back = lax.all_to_all(d_qkv_one, "space", 0, 0, tiled=True).reshape(8, 64, 1152)
-    first_all, middle_all = lax.optimization_barrier((first_all, middle_all))
+    give, middle_all = lax.optimization_barrier((give, middle_all))
     share = (share.astype(F32) + give.astype(F32)).astype(BF)
     column, = call(column_kernel, [((512, 192), BF)], (first_all, d_qkv_one), flops=2 * 10**9)
-    shares = jnp.concatenate([share, column], axis=1)
+    shares = jnp.concatenate([share, halve(column, 1, 0)], axis=1)
     shares, d_back = lax.optimization_barrier((shares, d_back))
     d_middle_mine = lax.dynamic_index_in_dim(
         middle_all.reshape(8, 6, 8, 8, 512), lax.axis_index("marker"), 2, keepdims=False
     )
     d_middle_mine = jnp.transpose(d_middle_mine, (1, 0, 2, 3)).reshape(384, 512)
-    shares = lax.all_to_all(shares, rows, 0, 0, tiled=True).reshape(8, 8, 8, 832).astype(F32)
-    column = jnp.sum(shares[..., 640:], axis=0).transpose(1, 0, 2).reshape(8, 1536)
+    shares = lax.all_to_all(shares, rows, 0, 0, tiled=True).reshape(8, 8, 8, 736).astype(F32)
+    column = jnp.sum(shares[..., 640:], axis=0).transpose(1, 0, 2).reshape(8, 768)
     share = jnp.sum(shares[..., :640], axis=(0, 1))
     share = jnp.concatenate([share, column], axis=1).astype(BF)
     share = lax.all_gather(share, "batch", axis=0, tiled=False)
-    share = share.reshape(2, 2, 8, 2176).astype(F32)
-    column = jnp.sum(share[..., 640:], axis=(0, 1))
+    share = share.reshape(2, 2, 8, 1408).astype(F32)
+    column = jnp.sum(share[..., 640:], axis=0).reshape(2, 8, 8, 96)
+    column = column.transpose(1, 2, 0, 3).reshape(8, 1536)
     share = share[..., :640].transpose(2, 1, 0, 3).reshape(8, 2560)
     d_tokens, = call(
         last_kernel, [((384, 512), BF)], (d_back, w_qkv_space, mine, gain_1, d_middle_mine),

time: 197 us -> 191 us (0.970)
  waiting for transfers between devices: 57 us -> 50.6 us
    all_gather x1, waiting for transfers between devices: 10.8 us -> 3.37 us  [on_device(): middle_all = lax.all_gather(d_middle, 'marker', axis=0, tiled=False)]
    all_to_all x1, waiting for transfers between devices: 0.01 us -> 3.52 us  [on_device(): lax.all_to_all(d_qkv_one, 'space', 0, 0, tiled=True).reshape(8, 64, 1152)]
    all_to_all x1, waiting for transfers between devices: 19 us -> 15.7 us  [on_device(): lax.all_to_all(shares, rows, 0, 0, tiled=True).reshape(8, 8, 8, 736)]
    all_to_all x1, starting transfers between devices: 9.89 us -> 7.61 us  [on_device(): lax.all_to_all(shares, rows, 0, 0, tiled=True).reshape(8, 8, 8, 736)]
    ppermute x2 -> x3, starting transfers between devices: 4.39 us -> 5.71 us  [swapped(): return lax.ppermute(x, 'batch', [(i, i ^ bit) for i in range(n)])]
  transfers between devices with their start and end apart: 16 -> 17, of which waited for: 6 -> 8; matrix products, arithmetic and copies ran while one was open for 7% -> 8% of each run, Pallas kernels for 17% -> 17%
where the time goes in v3:
time: 191 us; the launch traced here: 190 us
  starting transfers between devices  58.1 us (30%)
  waiting for transfers between devices  50.6 us (26%)
  Pallas kernels  36.3 us (19%)
  between operations  14.3 us (7%)
  local copies, waits for them, and re-layouts  10.7 us (6%)
  other arithmetic  9.92 us (5%)
  blocking collectives  9.88 us (5%)
    pallas_call x6, Pallas kernels, call(): pl.pallas_call(kernel, out_shape=[jax.ShapeDtypeStruct(shape, dtype) for...  36.3 us
    ppermute x7, starting transfers between devices, to_markers(): got = lax.ppermute(give, 'marker', [(i, (i + step) % n) for i in range(n)])  15.8 us
    all_to_all x1, waiting for transfers between devices, on_device(): lax.all_to_all(shares, rows, 0, 0, tiled=True).reshape(8, 8, 8, 736)  15.7 us
    all_to_all x1, waiting for transfers between devices, on_device(): d_heads = lax.all_to_all(d_send.reshape(512, 384), both, 0, 0, tiled=True)  11.8 us
    all_to_all x1, starting transfers between devices, on_device(): got = lax.all_to_all(heads, both, 0, 0, tiled=True).reshape(8, 64, 384)  11 us
    all_to_all x1, waiting for transfers between devices, on_device(): got = lax.all_to_all(heads, both, 0, 0, tiled=True).reshape(8, 64, 384)  10.5 us
    all_gather x1, blocking collectives, on_device(): share = lax.all_gather(share, 'batch', axis=0, tiled=False)  9.88 us
    all_to_all x1, starting transfers between devices, on_device(): lax.all_to_all(shares, rows, 0, 0, tiled=True).reshape(8, 8, 8, 736)  7.61 us
  transfers between devices with their start and end apart: 17, of which 8 were waited for; matrix products, arithmetic and copies ran while one was open for 8% of the time, Pallas kernels for 17%

profile of v3, /device:TPU:1, one launch (start us, length us, event | category | flops | bytes accessed | tf_op | source)
XLA Modules:
  0.0 189.9 jit_solution(13043718093999075170)
XLA Ops:
  7.2 3.7 %shard_map.135 = (bf16[512,384]{1,0:T(8,128)(2,1)}, bf16[8,64,1152]{2,1,0:T(8,128)(2,1)}) custom-call(bf16[384,512]{1,0:T(8,128)(2,1)} %bitcast.52, f32[1,512]{1,0:T(1,128)} %bitcast.61, bf16[512,1536]{1,0:T(8,128)(2,1)} %w_ref.3), custom_call_target="tpu_custom_call" | custom-call | flops 1000000000 | bytes 4000000 | tf_op jit(solution)/shard_map/pallas_call | solution.py:311
  10.9 7.6 %all-to-all-start = ((bf16[8,64,1152]{2,1,0:T(8,128)(2,1)}), bf16[8,64,1152]{2,1,0:T(8,128)(2,1)S(1)}, u32[]{:S(2)}, u32[]{:S(2)}) async-start(bf16[8,64,1152]{2,1,0:T(8,128)(2,1)} %get-tuple-element.27), calls=%async_computation | async-start | bytes 2359296 | tf_op jit(solution)/shard_map/all_to_all | solution.py:370
  18.6 7.0 %collective-permute-start = (bf16[2,6,1,8,512]{4,3,2,1,0:T(8,128)(2,1)S(1)}, bf16[2,6,1,8,512]{4,3,2,1,0:T(8,128)(2,1)S(1)}, u32[]{:S(2)}, u32[]{:S(2)}) collective-permute-start(bf16[2,6,1,8,512]{4,3,2,1,0:T(8,128)(2,1)S(1)} %get-tuple-element.52), channel_id=1, source_target_pairs={{0,32},{8,40},{16,48},{24,56},{32,0},{40,8},{48,16},{56,24},{1,33}... | collective-permute-start | bytes 294920 | tf_op jit(solution)/shard_map/ppermute | solution.py:332
  25.7 1.6 collective-permute-start.1
  27.3 2.8 %collective-permute-start.2 = (bf16[2,6,1,8,512]{4,3,2,1,0:T(8,128)(2,1)S(1)}, bf16[2,6,1,8,512]{4,3,2,1,0:T(8,128)(2,1)}, u32[]{:S(2)}, u32[]{:S(2)}) collective-permute-start(bf16[2,6,1,8,512]{4,3,2,1,0:T(8,128)(2,1)S(1)} %get-tuple-element.54), channel_id=1, source_target_pairs={{0,40},{8,48},{16,56},{24,0},{32,8},{40,16},{48,24},{56,32},{1,41}... | collective-permute-start | bytes 294920 | tf_op jit(solution)/shard_map/ppermute | solution.py:332
  31.3 2.4 %collective-permute-start.4 = (bf16[2,6,1,8,512]{4,3,2,1,0:T(8,128)(2,1)S(1)}, bf16[2,6,1,8,512]{4,3,2,1,0:T(8,128)(2,1)}, u32[]{:S(2)}, u32[]{:S(2)}) collective-permute-start(bf16[2,6,1,8,512]{4,3,2,1,0:T(8,128)(2,1)S(1)} %get-tuple-element.56), channel_id=1, source_target_pairs={{0,48},{8,56},{16,0},{24,8},{32,16},{40,24},{48,32},{56,40},{1,49}... | collective-permute-start | bytes 294920 | tf_op jit(solution)/shard_map/ppermute | solution.py:332
  35.2 3.9 %collective-permute-done.1 = bf16[2,6,1,8,512]{4,3,2,1,0:T(8,128)(2,1)S(1)} collective-permute-done((bf16[2,6,1,8,512]{4,3,2,1,0:T(8,128)(2,1)S(1)}, bf16[2,6,1,8,512]{4,3,2,1,0:T(8,128)(2,1)S(1)}, u32[]{:S(2)}, u32[]{:S(2)}) %collective-permute-start.1) | collective-permute-done | bytes 98336 | tf_op jit(solution)/shard_map/ppermute | solution.py:332
  39.9 4.5 %shard_map.136 = (bf16[512,384]{1,0:T(8,128)(2,1)}, f32[6,512]{1,0:T(8,128)S(1)}) custom-call(bf16[512,1152]{1,0:T(8,128)(2,1)S(1)} %bitcast.57), custom_call_target="tpu_custom_call" | custom-call | flops 2000000000 | bytes 4000000 | tf_op jit(solution)/shard_map/pallas_call | solution.py:311
  44.4 11.0 %all-to-all-start.1 = ((bf16[64,8,384]{2,1,0:T(8,128)(2,1)}), bf16[64,8,384]{2,1,0:T(8,128)(2,1)S(1)}, u32[]{:S(2)}, u32[]{:S(2)}) async-start(bf16[64,8,384]{2,1,0:T(8,128)(2,1)} %bitcast.6), calls=%async_computation.1 | async-start | bytes 786432 | tf_op jit(solution)/shard_map/all_to_all | solution.py:378
  59.4 10.5 %all-to-all-done.1 = bf16[64,8,384]{2,1,0:T(8,128)(2,1)S(1)} async-done(((bf16[64,8,384]{2,1,0:T(8,128)(2,1)}), bf16[64,8,384]{2,1,0:T(8,128)(2,1)S(1)}, u32[]{:S(2)}, u32[]{:S(2)}) %all-to-all-start.1) | async-done | bytes 393248 | tf_op jit(solution)/shard_map/all_to_all | solution.py:378
  70.7 13.4 %shard_map.137 = (bf16[512,1280]{1,0:T(8,128)(2,1)}, bf16[512,1280]{1,0:T(8,128)(2,1)}, bf16[384,512]{1,0:T(8,128)(2,1)}, bf16[8,64,384]{2,1,0:T(8,128)(2,1)}) custom-call(s32[1]{0:T(128)} %bitcast.core_ref, bf16[8,64,384]{2,1,0:T(8,128)(2,1)} %bitcast.68, bf16[384,512]{1,0:T(8,128)(2,1)} %bitcast.71, bf16[384,512]{1,0:T(8,128)(2,1)} %bitcast.70, ...), custom_call_target="tpu_custom_call" | custom-call | flops 6000000000 | bytes 4000000 | tf_op jit(solution)/shard_map/pallas_call | solution.py:311
  84.1 4.2 %collective-permute-start.7 = (bf16[512,1280]{1,0:T(8,128)(2,1)}, bf16[512,1280]{1,0:T(8,128)(2,1)S(1)}, u32[]{:S(2)}, u32[]{:S(2)}) collective-permute-start(bf16[512,1280]{1,0:T(8,128)(2,1)} %get-tuple-element.30), channel_id=1, source_target_pairs={{0,64},{64,0},{128,192},{192,128},{1,65},{65,1},{129,193},{193,129... | collective-permute-start | bytes 3932168 | tf_op jit(solution)/shard_map/ppermute | solution.py:339
  88.3 4.6 %all-to-all-start.2 = ((bf16[64,8,384]{2,1,0:T(8,128)(2,1)}), bf16[64,8,384]{2,1,0:T(8,128)(2,1)S(1)}, u32[]{:S(2)}, u32[]{:S(2)}) async-start(bf16[64,8,384]{2,1,0:T(8,128)(2,1)} %bitcast.69), calls=%async_computation.2 | async-start | bytes 786432 | tf_op jit(solution)/shard_map/all_to_all | solution.py:392
  94.1 2.0 %add_convert_fusion = bf16[512,1280]{1,0:T(8,128)(2,1)S(1)} fusion(bf16[512,1280]{1,0:T(8,128)(2,1)} %copy-done.4, bf16[512,1280]{1,0:T(8,128)(2,1)} %get-tuple-element.29), kind=kLoop, calls=%fused_computation | loop fusion | flops 2621440 | bytes 3932160 | tf_op jit(solution)/shard_map/convert_element_type | solution.py:400
  97.2 11.8 %all-to-all-done.2 = bf16[64,8,384]{2,1,0:T(8,128)(2,1)S(1)} async-done(((bf16[64,8,384]{2,1,0:T(8,128)(2,1)}), bf16[64,8,384]{2,1,0:T(8,128)(2,1)S(1)}, u32[]{:S(2)}, u32[]{:S(2)}) %all-to-all-start.2) | async-done | bytes 393248 | tf_op jit(solution)/shard_map/all_to_all | solution.py:392
  109.0 7.7 %shard_map.138.d_qkv_ref = bf16[512,1152]{1,0:T(8,128)(2,1)} custom-call(bf16[512,1152]{1,0:T(8,128)(2,1)S(1)} %bitcast.58, bf16[512,384]{1,0:T(8,128)(2,1)} %get-tuple-element.28.heads_ref, f32[6,512]{1,0:T(8,128)S(1)} %get-tuple-element.31.inv_ref, bf16[512,384]{1,0:T(8,128)(2,1)S(1)} %bitcast.59), custom_call_target="tpu_custom_call" | custom-call | flops 1000000 | bytes 10000 | tf_op jit(solution)/shard_map/pallas_call | solution.py:311
  116.8 5.5 %all-to-all-start.3 = ((bf16[8,64,1152]{2,1,0:T(8,128)(2,1)}), bf16[8,64,1152]{2,1,0:T(8,128)(2,1)S(1)}, u32[]{:S(2)}, u32[]{:S(2)}) async-start(bf16[8,64,1152]{2,1,0:T(8,128)(2,1)} %bitcast.20), calls=%async_computation.3 | async-start | bytes 2359296 | tf_op jit(solution)/shard_map/all_to_all | solution.py:403
  122.3 5.2 %shard_map.139 = bf16[512,192]{1,0:T(8,128)(2,1)} custom-call(bf16[8,512,384]{2,1,0:T(8,128)(2,1)} %bitcast.76, bf16[512,1152]{1,0:T(8,128)(2,1)} %shard_map.138.d_qkv_ref), custom_call_target="tpu_custom_call" | custom-call | flops 2000000000 | bytes 4000000 | tf_op jit(solution)/shard_map/pallas_call | solution.py:311
  131.9 3.4 %all-gather.7.cloned.1.call-done = bf16[3072,512]{1,0:T(8,128)(2,1)} async-done(((bf16[384,512]{1,0:T(8,128)(2,1)}), bf16[3072,512]{1,0:T(8,128)(2,1)}) %all-gather.7.cloned.1.call-update) | async-done | bytes 3145744 | tf_op jit(solution)/shard_map/all_gather | solution.py:399
  137.5 3.5 %all-to-all-done.3.got_ref = bf16[8,64,1152]{2,1,0:T(8,128)(2,1)S(1)} async-done(((bf16[8,64,1152]{2,1,0:T(8,128)(2,1)}), bf16[8,64,1152]{2,1,0:T(8,128)(2,1)S(1)}, u32[]{:S(2)}, u32[]{:S(2)}) %all-to-all-start.3) | async-done | bytes 1179680 | tf_op jit(solution)/shard_map/all_to_all | solution.py:403
  141.0 7.6 %all-to-all-start.4 = ((bf16[64,8,736]{2,1,0:T(8,128)(2,1)}), bf16[64,8,736]{2,1,0:T(8,128)(2,1)}, u32[]{:S(2)}, u32[]{:S(2)}) async-start(bf16[64,8,736]{2,1,0:T(8,128)(2,1)} %bitcast.66), calls=%async_computation.4 | async-start | bytes 1572864 | tf_op jit(solution)/shard_map/all_to_all | solution.py:413
  151.2 1.8 shard_map.140
  153.0 15.7 %all-to-all-done.4 = bf16[64,8,736]{2,1,0:T(8,128)(2,1)} async-done(((bf16[64,8,736]{2,1,0:T(8,128)(2,1)}), bf16[64,8,736]{2,1,0:T(8,128)(2,1)}, u32[]{:S(2)}, u32[]{:S(2)}) %all-to-all-start.4) | async-done | bytes 753696 | tf_op jit(solution)/shard_map/all_to_all | solution.py:413
  170.2 9.9 %all_gather.20 = bf16[4,8,1408]{2,1,0:T(8,128)(2,1)S(1)} all-gather(bf16[1,8,1408]{2,1,0:T(8,128)(2,1)S(1)} %pad_maximum_fusion.2), channel_id=1, replica_groups=mesh['batch'=4,'marker'=8,'space'=8] {'batch'}, dimensions={0}, use_global_device_ids=true | all-gather | bytes 112640 | tf_op jit(solution)/shard_map/all_gather | solution.py:417
  (75 shorter events, 24.2 us)
Async XLA Ops:
  7.2 101.9 %all-gather.5.cloned.1.call-start = ((), (), s32[]{:S(2)}) async-start(), calls=%async_computation.5 | async-start | bytes 3538944 | tf_op jit(solution)/shard_map/all_gather | solution.py:372
  10.9 7.6 %copy-start = (bf16[1,64,6,512]{3,1,2,0:T(8,128)(2,1)S(1)}, bf16[1,64,6,512]{3,1,2,0:T(8,128)(2,1)}, u32[]{:S(2)}) copy-start(bf16[1,64,6,512]{3,1,2,0:T(8,128)(2,1)} %param.8) | copy-start | bytes 1179652
  10.9 7.6 %copy-start.3 = (bf16[1,64,6,512]{3,1,2,0:T(8,128)(2,1)S(1)}, bf16[1,64,6,512]{3,1,2,0:T(8,128)(2,1)}, u32[]{:S(2)}) copy-start(bf16[1,64,6,512]{3,1,2,0:T(8,128)(2,1)} %param.15) | copy-start | bytes 1179652
  10.9 29.0 %all-to-all-start = ((bf16[8,64,1152]{2,1,0:T(8,128)(2,1)}), bf16[8,64,1152]{2,1,0:T(8,128)(2,1)S(1)}, u32[]{:S(2)}, u32[]{:S(2)}) async-start(bf16[8,64,1152]{2,1,0:T(8,128)(2,1)} %get-tuple-element.27), calls=%async_computation | async-start | bytes 2359296 | tf_op jit(solution)/shard_map/all_to_all | solution.py:370
  18.6 15.8 %collective-permute-start = (bf16[2,6,1,8,512]{4,3,2,1,0:T(8,128)(2,1)S(1)}, bf16[2,6,1,8,512]{4,3,2,1,0:T(8,128)(2,1)S(1)}, u32[]{:S(2)}, u32[]{:S(2)}) collective-permute-start(bf16[2,6,1,8,512]{4,3,2,1,0:T(8,128)(2,1)S(1)} %get-tuple-element.52), channel_id=1, source_target_pairs={{0,32},{8,40},{16,48},{24,56},{32,0},{40,8},{48,16},{56,24},{1,33}... | collective-permute-start | bytes 294920 | tf_op jit(solution)/shard_map/ppermute | solution.py:332
  25.7 13.4 %collective-permute-start.1 = (bf16[2,6,1,8,512]{4,3,2,1,0:T(8,128)(2,1)S(1)}, bf16[2,6,1,8,512]{4,3,2,1,0:T(8,128)(2,1)S(1)}, u32[]{:S(2)}, u32[]{:S(2)}) collective-permute-start(bf16[2,6,1,8,512]{4,3,2,1,0:T(8,128)(2,1)S(1)} %get-tuple-element.53), channel_id=1, source_target_pairs={{0,24},{8,32},{16,40},{24,48},{32,56},{40,0},{48,8},{56,16},{1,25}... | collective-permute-start | bytes 294920 | tf_op jit(solution)/shard_map/ppermute | solution.py:332
  27.3 28.4 %collective-permute-start.2 = (bf16[2,6,1,8,512]{4,3,2,1,0:T(8,128)(2,1)S(1)}, bf16[2,6,1,8,512]{4,3,2,1,0:T(8,128)(2,1)}, u32[]{:S(2)}, u32[]{:S(2)}) collective-permute-start(bf16[2,6,1,8,512]{4,3,2,1,0:T(8,128)(2,1)S(1)} %get-tuple-element.54), channel_id=1, source_target_pairs={{0,40},{8,48},{16,56},{24,0},{32,8},{40,16},{48,24},{56,32},{1,41}... | collective-permute-start | bytes 294920 | tf_op jit(solution)/shard_map/ppermute | solution.py:332
  30.1 26.5 %collective-permute-start.3 = (bf16[2,6,1,8,512]{4,3,2,1,0:T(8,128)(2,1)S(1)}, bf16[2,6,1,8,512]{4,3,2,1,0:T(8,128)(2,1)}, u32[]{:S(2)}, u32[]{:S(2)}) collective-permute-start(bf16[2,6,1,8,512]{4,3,2,1,0:T(8,128)(2,1)S(1)} %get-tuple-element.55), channel_id=1, source_target_pairs={{0,16},{8,24},{16,32},{24,40},{32,48},{40,56},{48,0},{56,8},{1,17}... | collective-permute-start | bytes 294920 | tf_op jit(solution)/shard_map/ppermute | solution.py:332
  31.3 26.2 %collective-permute-start.4 = (bf16[2,6,1,8,512]{4,3,2,1,0:T(8,128)(2,1)S(1)}, bf16[2,6,1,8,512]{4,3,2,1,0:T(8,128)(2,1)}, u32[]{:S(2)}, u32[]{:S(2)}) collective-permute-start(bf16[2,6,1,8,512]{4,3,2,1,0:T(8,128)(2,1)S(1)} %get-tuple-element.56), channel_id=1, source_target_pairs={{0,48},{8,56},{16,0},{24,8},{32,16},{40,24},{48,32},{56,40},{1,49}... | collective-permute-start | bytes 294920 | tf_op jit(solution)/shard_map/ppermute | solution.py:332
  34.4 24.0 %collective-permute-start.5 = (bf16[2,6,1,8,512]{4,3,2,1,0:T(8,128)(2,1)}, bf16[2,6,1,8,512]{4,3,2,1,0:T(8,128)(2,1)S(1)}, u32[]{:S(2)}, u32[]{:S(2)}) collective-permute-start(bf16[2,6,1,8,512]{4,3,2,1,0:T(8,128)(2,1)} %fusion.5), channel_id=1, source_target_pairs={{0,8},{8,16},{16,24},{24,32},{32,40},{40,48},{48,56},{56,0},{1,9},... | collective-permute-start | bytes 294920 | tf_op jit(solution)/shard_map/ppermute | solution.py:332
  39.1 19.4 %collective-permute-start.6 = (bf16[2,6,1,8,512]{4,3,2,1,0:T(8,128)(2,1)S(1)}, bf16[2,6,1,8,512]{4,3,2,1,0:T(8,128)(2,1)S(1)}, u32[]{:S(2)}, u32[]{:S(2)}) collective-permute-start(bf16[2,6,1,8,512]{4,3,2,1,0:T(8,128)(2,1)S(1)} %get-tuple-element.51), channel_id=1, source_target_pairs={{0,56},{8,0},{16,8},{24,16},{32,24},{40,32},{48,40},{56,48},{1,57}... | collective-permute-start | bytes 294920 | tf_op jit(solution)/shard_map/ppermute | solution.py:332
  44.4 25.5 %all-to-all-start.1 = ((bf16[64,8,384]{2,1,0:T(8,128)(2,1)}), bf16[64,8,384]{2,1,0:T(8,128)(2,1)S(1)}, u32[]{:S(2)}, u32[]{:S(2)}) async-start(bf16[64,8,384]{2,1,0:T(8,128)(2,1)} %bitcast.6), calls=%async_computation.1 | async-start | bytes 786432 | tf_op jit(solution)/shard_map/all_to_all | solution.py:378
  55.4 79.8 %all-gather.7.cloned.1.call-start = ((), (), s32[]{:S(2)}) async-start(), calls=%async_computation.6 | async-start | bytes 3538944 | tf_op jit(solution)/shard_map/all_gather | solution.py:399
  69.9 0.7 copy-start.5
  84.1 8.8 %collective-permute-start.7 = (bf16[512,1280]{1,0:T(8,128)(2,1)}, bf16[512,1280]{1,0:T(8,128)(2,1)S(1)}, u32[]{:S(2)}, u32[]{:S(2)}) collective-permute-start(bf16[512,1280]{1,0:T(8,128)(2,1)} %get-tuple-element.30), channel_id=1, source_target_pairs={{0,64},{64,0},{128,192},{192,128},{1,65},{65,1},{129,193},{193,129... | collective-permute-start | bytes 3932168 | tf_op jit(solution)/shard_map/ppermute | solution.py:339
  88.3 20.8 %all-to-all-start.2 = ((bf16[64,8,384]{2,1,0:T(8,128)(2,1)}), bf16[64,8,384]{2,1,0:T(8,128)(2,1)S(1)}, u32[]{:S(2)}, u32[]{:S(2)}) async-start(bf16[64,8,384]{2,1,0:T(8,128)(2,1)} %bitcast.69), calls=%async_computation.2 | async-start | bytes 786432 | tf_op jit(solution)/shard_map/all_to_all | solution.py:392
  92.9 1.1 copy-start.4
  97.0 19.8 %collective-permute-start.8 = (bf16[512,640]{1,0:T(8,128)(2,1)}, bf16[512,640]{1,0:T(8,128)(2,1)}, u32[]{:S(2)}, u32[]{:S(2)}) collective-permute-start(bf16[512,640]{1,0:T(8,128)(2,1)} %constant_dynamic-slice_fusion.4), channel_id=1, source_target_pairs={{0,128},{64,192},{128,0},{192,64},{1,129},{65,193},{129,1},{193,65... | collective-permute-start | bytes 1966088 | tf_op jit(solution)/shard_map/ppermute | solution.py:339
  116.8 24.2 %all-to-all-start.3 = ((bf16[8,64,1152]{2,1,0:T(8,128)(2,1)}), bf16[8,64,1152]{2,1,0:T(8,128)(2,1)S(1)}, u32[]{:S(2)}, u32[]{:S(2)}) async-start(bf16[8,64,1152]{2,1,0:T(8,128)(2,1)} %bitcast.20), calls=%async_computation.3 | async-start | bytes 2359296 | tf_op jit(solution)/shard_map/all_to_all | solution.py:403
  128.5 2.3 %collective-permute-start.9 = (bf16[512,96]{1,0:T(8,128)(2,1)S(1)}, bf16[512,96]{1,0:T(8,128)(2,1)S(1)}, u32[]{:S(2)}, u32[]{:S(2)}) collective-permute-start(bf16[512,96]{1,0:T(8,128)(2,1)S(1)} %constant_dynamic-slice_fusion.3), channel_id=1, source_target_pairs={{0,64},{64,0},{128,192},{192,128},{1,65},{65,1},{129,193},{193,129... | collective-permute-start | bytes 294920 | tf_op jit(solution)/shard_map/ppermute | solution.py:339
  136.5 12.1 %copy-start.2 = (f32[512]{0:T(512)S(1)}, f32[512]{0:T(512)}, u32[]{:S(2)}) copy-start(f32[512]{0:T(512)} %param.9) | copy-start | bytes 6148
  136.5 13.0 %copy-start.1 = (bf16[512,1536]{1,0:T(8,128)(2,1)S(1)}, bf16[512,1536]{1,0:T(8,128)(2,1)}, u32[]{:S(2)}) copy-start(bf16[512,1536]{1,0:T(8,128)(2,1)} %w_ref.3) | copy-start | bytes 4718596
  141.0 27.7 %all-to-all-start.4 = ((bf16[64,8,736]{2,1,0:T(8,128)(2,1)}), bf16[64,8,736]{2,1,0:T(8,128)(2,1)}, u32[]{:S(2)}, u32[]{:S(2)}) async-start(bf16[64,8,736]{2,1,0:T(8,128)(2,1)} %bitcast.66), calls=%async_computation.4 | async-start | bytes 1572864 | tf_op jit(solution)/shard_map/all_to_all | solution.py:413
  180.5 2.6 %copy-start.6 = (f32[8,1536]{1,0:T(8,128)}, f32[8,1536]{1,0:T(8,128)S(1)}, u32[]{:S(2)}) copy-start(f32[8,1536]{1,0:T(8,128)S(1)} %mul.52) | copy-start | bytes 147460
Sparse Core Ops, SparseCore 0:
  11.2 79.3 all-gather.4
  92.3 42.8 all-gather.6

commit v4 on v3

--- a/solution.py
+++ b/solution.py
@@ -103,7 +103,7 @@
 def spatial_kernel(qkv_ref, heads_ref, inv_ref):
     length = qkv_ref.shape[0]
     lo = low_half(length)
-    step = 256
+    step = 512
     for jj in range(3):
         at = jj * 384
         query = qkv_ref[:, at : at + 128].astype(F32)
@@ -129,7 +129,7 @@
 def spatial_back_kernel(qkv_ref, heads_ref, inv_ref, d_heads_ref, d_qkv_ref):
     length = qkv_ref.shape[0]
     lo = low_half(length)
-    step = 256
+    step = 512
     for jj in range(3):
         at = jj * 384
         query = qkv_ref[:, at : at + 128].astype(F32)

time: 191 us -> 190 us (level)
  transfers between devices with their start and end apart: 17 -> 17, of which waited for: 8 -> 9; matrix products, arithmetic and copies ran while one was open for 8% -> 8% of each run, Pallas kernels for 17% -> 16%
where the time goes in v4:
time: 190 us; the launch traced here: 189 us
  starting transfers between devices  58.3 us (31%)
  waiting for transfers between devices  51.1 us (27%)
  Pallas kernels  34.5 us (18%)
  between operations  14.3 us (8%)
  local copies, waits for them, and re-layouts  10.7 us (6%)
  other arithmetic  9.92 us (5%)
  blocking collectives  9.88 us (5%)
    pallas_call x6, Pallas kernels, call(): pl.pallas_call(kernel, out_shape=[jax.ShapeDtypeStruct(shape, dtype) for...  34.5 us
    ppermute x7, starting transfers between devices, to_markers(): got = lax.ppermute(give, 'marker', [(i, (i + step) % n) for i in range(n)])  15.8 us
    all_to_all x1, waiting for transfers between devices, on_device(): lax.all_to_all(shares, rows, 0, 0, tiled=True).reshape(8, 8, 8, 736)  15.7 us
    all_to_all x1, waiting for transfers between devices, on_device(): d_heads = lax.all_to_all(d_send.reshape(512, 384), both, 0, 0, tiled=True)  11.9 us
    all_to_all x1, starting transfers between devices, on_device(): got = lax.all_to_all(heads, both, 0, 0, tiled=True).reshape(8, 64, 384)  11 us
    all_to_all x1, waiting for transfers between devices, on_device(): got = lax.all_to_all(heads, both, 0, 0, tiled=True).reshape(8, 64, 384)  10.5 us
    all_gather x1, blocking collectives, on_device(): share = lax.all_gather(share, 'batch', axis=0, tiled=False)  9.88 us
    all_to_all x1, starting transfers between devices, on_device(): lax.all_to_all(shares, rows, 0, 0, tiled=True).reshape(8, 8, 8, 736)  7.63 us
  transfers between devices with their start and end apart: 17, of which 9 were waited for; matrix products, arithmetic and copies ran while one was open for 8% of the time, Pallas kernels for 16%

profile of v4, /device:TPU:1, one launch (start us, length us, event | category | flops | bytes accessed | tf_op | source)
XLA Modules:
  0.0 188.8 jit_solution(11715119967168572936)
XLA Ops:
  7.2 3.7 %shard_map.135 = (bf16[512,384]{1,0:T(8,128)(2,1)}, bf16[8,64,1152]{2,1,0:T(8,128)(2,1)}) custom-call(bf16[384,512]{1,0:T(8,128)(2,1)} %bitcast.52, f32[1,512]{1,0:T(1,128)} %bitcast.61, bf16[512,1536]{1,0:T(8,128)(2,1)} %w_ref.3), custom_call_target="tpu_custom_call" | custom-call | flops 1000000000 | bytes 4000000 | tf_op jit(solution)/shard_map/pallas_call | solution.py:311
  10.9 7.6 %all-to-all-start = ((bf16[8,64,1152]{2,1,0:T(8,128)(2,1)}), bf16[8,64,1152]{2,1,0:T(8,128)(2,1)S(1)}, u32[]{:S(2)}, u32[]{:S(2)}) async-start(bf16[8,64,1152]{2,1,0:T(8,128)(2,1)} %get-tuple-element.27), calls=%async_computation | async-start | bytes 2359296 | tf_op jit(solution)/shard_map/all_to_all | solution.py:370
  18.6 7.0 %collective-permute-start = (bf16[2,6,1,8,512]{4,3,2,1,0:T(8,128)(2,1)S(1)}, bf16[2,6,1,8,512]{4,3,2,1,0:T(8,128)(2,1)S(1)}, u32[]{:S(2)}, u32[]{:S(2)}) collective-permute-start(bf16[2,6,1,8,512]{4,3,2,1,0:T(8,128)(2,1)S(1)} %get-tuple-element.52), channel_id=1, source_target_pairs={{0,32},{8,40},{16,48},{24,56},{32,0},{40,8},{48,16},{56,24},{1,33}... | collective-permute-start | bytes 294920 | tf_op jit(solution)/shard_map/ppermute | solution.py:332
  25.7 1.6 collective-permute-start.1
  27.3 2.8 %collective-permute-start.2 = (bf16[2,6,1,8,512]{4,3,2,1,0:T(8,128)(2,1)S(1)}, bf16[2,6,1,8,512]{4,3,2,1,0:T(8,128)(2,1)}, u32[]{:S(2)}, u32[]{:S(2)}) collective-permute-start(bf16[2,6,1,8,512]{4,3,2,1,0:T(8,128)(2,1)S(1)} %get-tuple-element.54), channel_id=1, source_target_pairs={{0,40},{8,48},{16,56},{24,0},{32,8},{40,16},{48,24},{56,32},{1,41}... | collective-permute-start | bytes 294920 | tf_op jit(solution)/shard_map/ppermute | solution.py:332
  31.3 2.4 %collective-permute-start.4 = (bf16[2,6,1,8,512]{4,3,2,1,0:T(8,128)(2,1)S(1)}, bf16[2,6,1,8,512]{4,3,2,1,0:T(8,128)(2,1)}, u32[]{:S(2)}, u32[]{:S(2)}) collective-permute-start(bf16[2,6,1,8,512]{4,3,2,1,0:T(8,128)(2,1)S(1)} %get-tuple-element.56), channel_id=1, source_target_pairs={{0,48},{8,56},{16,0},{24,8},{32,16},{40,24},{48,32},{56,40},{1,49}... | collective-permute-start | bytes 294920 | tf_op jit(solution)/shard_map/ppermute | solution.py:332
  35.2 3.9 %collective-permute-done.1 = bf16[2,6,1,8,512]{4,3,2,1,0:T(8,128)(2,1)S(1)} collective-permute-done((bf16[2,6,1,8,512]{4,3,2,1,0:T(8,128)(2,1)S(1)}, bf16[2,6,1,8,512]{4,3,2,1,0:T(8,128)(2,1)S(1)}, u32[]{:S(2)}, u32[]{:S(2)}) %collective-permute-start.1) | collective-permute-done | bytes 98336 | tf_op jit(solution)/shard_map/ppermute | solution.py:332
  39.9 3.3 %shard_map.136 = (bf16[512,384]{1,0:T(8,128)(2,1)}, f32[6,512]{1,0:T(8,128)S(1)}) custom-call(bf16[512,1152]{1,0:T(8,128)(2,1)S(1)} %bitcast.57), custom_call_target="tpu_custom_call" | custom-call | flops 2000000000 | bytes 4000000 | tf_op jit(solution)/shard_map/pallas_call | solution.py:311
  43.2 11.0 %all-to-all-start.1 = ((bf16[64,8,384]{2,1,0:T(8,128)(2,1)}), bf16[64,8,384]{2,1,0:T(8,128)(2,1)S(1)}, u32[]{:S(2)}, u32[]{:S(2)}) async-start(bf16[64,8,384]{2,1,0:T(8,128)(2,1)} %bitcast.6), calls=%async_computation.1 | async-start | bytes 786432 | tf_op jit(solution)/shard_map/all_to_all | solution.py:378
  58.2 10.5 %all-to-all-done.1 = bf16[64,8,384]{2,1,0:T(8,128)(2,1)S(1)} async-done(((bf16[64,8,384]{2,1,0:T(8,128)(2,1)}), bf16[64,8,384]{2,1,0:T(8,128)(2,1)S(1)}, u32[]{:S(2)}, u32[]{:S(2)}) %all-to-all-start.1) | async-done | bytes 393248 | tf_op jit(solution)/shard_map/all_to_all | solution.py:378
  69.5 13.4 %shard_map.137 = (bf16[512,1280]{1,0:T(8,128)(2,1)}, bf16[512,1280]{1,0:T(8,128)(2,1)}, bf16[384,512]{1,0:T(8,128)(2,1)}, bf16[8,64,384]{2,1,0:T(8,128)(2,1)}) custom-call(s32[1]{0:T(128)} %bitcast.core_ref, bf16[8,64,384]{2,1,0:T(8,128)(2,1)} %bitcast.68, bf16[384,512]{1,0:T(8,128)(2,1)} %bitcast.71, bf16[384,512]{1,0:T(8,128)(2,1)} %bitcast.70, ...), custom_call_target="tpu_custom_call" | custom-call | flops 6000000000 | bytes 4000000 | tf_op jit(solution)/shard_map/pallas_call | solution.py:311
  82.9 4.2 %collective-permute-start.7 = (bf16[512,1280]{1,0:T(8,128)(2,1)}, bf16[512,1280]{1,0:T(8,128)(2,1)S(1)}, u32[]{:S(2)}, u32[]{:S(2)}) collective-permute-start(bf16[512,1280]{1,0:T(8,128)(2,1)} %get-tuple-element.30), channel_id=1, source_target_pairs={{0,64},{64,0},{128,192},{192,128},{1,65},{65,1},{129,193},{193,129... | collective-permute-start | bytes 3932168 | tf_op jit(solution)/shard_map/ppermute | solution.py:339
  87.1 4.6 %all-to-all-start.2 = ((bf16[64,8,384]{2,1,0:T(8,128)(2,1)}), bf16[64,8,384]{2,1,0:T(8,128)(2,1)S(1)}, u32[]{:S(2)}, u32[]{:S(2)}) async-start(bf16[64,8,384]{2,1,0:T(8,128)(2,1)} %bitcast.69), calls=%async_computation.2 | async-start | bytes 786432 | tf_op jit(solution)/shard_map/all_to_all | solution.py:392
  92.9 2.0 %add_convert_fusion = bf16[512,1280]{1,0:T(8,128)(2,1)S(1)} fusion(bf16[512,1280]{1,0:T(8,128)(2,1)} %copy-done.4, bf16[512,1280]{1,0:T(8,128)(2,1)} %get-tuple-element.29), kind=kLoop, calls=%fused_computation | loop fusion | flops 2621440 | bytes 3932160 | tf_op jit(solution)/shard_map/convert_element_type | solution.py:400
  96.1 11.9 %all-to-all-done.2 = bf16[64,8,384]{2,1,0:T(8,128)(2,1)S(1)} async-done(((bf16[64,8,384]{2,1,0:T(8,128)(2,1)}), bf16[64,8,384]{2,1,0:T(8,128)(2,1)S(1)}, u32[]{:S(2)}, u32[]{:S(2)}) %all-to-all-start.2) | async-done | bytes 393248 | tf_op jit(solution)/shard_map/all_to_all | solution.py:392
  108.0 7.1 %shard_map.138.d_qkv_ref = bf16[512,1152]{1,0:T(8,128)(2,1)} custom-call(bf16[512,1152]{1,0:T(8,128)(2,1)S(1)} %bitcast.58, bf16[512,384]{1,0:T(8,128)(2,1)} %get-tuple-element.28.heads_ref, f32[6,512]{1,0:T(8,128)S(1)} %get-tuple-element.31.inv_ref, bf16[512,384]{1,0:T(8,128)(2,1)S(1)} %bitcast.59), custom_call_target="tpu_custom_call" | custom-call | flops 1000000 | bytes 10000 | tf_op jit(solution)/shard_map/pallas_call | solution.py:311
  115.4 5.7 %all-to-all-start.3 = ((bf16[8,64,1152]{2,1,0:T(8,128)(2,1)}), bf16[8,64,1152]{2,1,0:T(8,128)(2,1)S(1)}, u32[]{:S(2)}, u32[]{:S(2)}) async-start(bf16[8,64,1152]{2,1,0:T(8,128)(2,1)} %bitcast.20), calls=%async_computation.3 | async-start | bytes 2359296 | tf_op jit(solution)/shard_map/all_to_all | solution.py:403
  121.1 5.2 %shard_map.139 = bf16[512,192]{1,0:T(8,128)(2,1)} custom-call(bf16[8,512,384]{2,1,0:T(8,128)(2,1)} %bitcast.76, bf16[512,1152]{1,0:T(8,128)(2,1)} %shard_map.138.d_qkv_ref), custom_call_target="tpu_custom_call" | custom-call | flops 2000000000 | bytes 4000000 | tf_op jit(solution)/shard_map/pallas_call | solution.py:311
  130.7 3.7 %all-gather.7.cloned.1.call-done = bf16[3072,512]{1,0:T(8,128)(2,1)} async-done(((bf16[384,512]{1,0:T(8,128)(2,1)}), bf16[3072,512]{1,0:T(8,128)(2,1)}) %all-gather.7.cloned.1.call-update) | async-done | bytes 3145744 | tf_op jit(solution)/shard_map/all_gather | solution.py:399
  136.6 3.3 %all-to-all-done.3.got_ref = bf16[8,64,1152]{2,1,0:T(8,128)(2,1)S(1)} async-done(((bf16[8,64,1152]{2,1,0:T(8,128)(2,1)}), bf16[8,64,1152]{2,1,0:T(8,128)(2,1)S(1)}, u32[]{:S(2)}, u32[]{:S(2)}) %all-to-all-start.3) | async-done | bytes 1179680 | tf_op jit(solution)/shard_map/all_to_all | solution.py:403
  139.8 7.6 %all-to-all-start.4 = ((bf16[64,8,736]{2,1,0:T(8,128)(2,1)}), bf16[64,8,736]{2,1,0:T(8,128)(2,1)}, u32[]{:S(2)}, u32[]{:S(2)}) async-start(bf16[64,8,736]{2,1,0:T(8,128)(2,1)} %bitcast.66), calls=%async_computation.4 | async-start | bytes 1572864 | tf_op jit(solution)/shard_map/all_to_all | solution.py:413
  150.1 1.8 shard_map.140
  151.9 15.7 %all-to-all-done.4 = bf16[64,8,736]{2,1,0:T(8,128)(2,1)} async-done(((bf16[64,8,736]{2,1,0:T(8,128)(2,1)}), bf16[64,8,736]{2,1,0:T(8,128)(2,1)}, u32[]{:S(2)}, u32[]{:S(2)}) %all-to-all-start.4) | async-done | bytes 753696 | tf_op jit(solution)/shard_map/all_to_all | solution.py:413
  169.1 9.9 %all_gather.20 = bf16[4,8,1408]{2,1,0:T(8,128)(2,1)S(1)} all-gather(bf16[1,8,1408]{2,1,0:T(8,128)(2,1)S(1)} %pad_maximum_fusion.2), channel_id=1, replica_groups=mesh['batch'=4,'marker'=8,'space'=8] {'batch'}, dimensions={0}, use_global_device_ids=true | all-gather | bytes 112640 | tf_op jit(solution)/shard_map/all_gather | solution.py:417
  (75 shorter events, 24.5 us)
Async XLA Ops:
  7.2 100.8 %all-gather.5.cloned.1.call-start = ((), (), s32[]{:S(2)}) async-start(), calls=%async_computation.5 | async-start | bytes 3538944 | tf_op jit(solution)/shard_map/all_gather | solution.py:372
  10.9 7.6 %copy-start = (bf16[1,64,6,512]{3,1,2,0:T(8,128)(2,1)S(1)}, bf16[1,64,6,512]{3,1,2,0:T(8,128)(2,1)}, u32[]{:S(2)}) copy-start(bf16[1,64,6,512]{3,1,2,0:T(8,128)(2,1)} %param.8) | copy-start | bytes 1179652
  10.9 7.6 %copy-start.3 = (bf16[1,64,6,512]{3,1,2,0:T(8,128)(2,1)S(1)}, bf16[1,64,6,512]{3,1,2,0:T(8,128)(2,1)}, u32[]{:S(2)}) copy-start(bf16[1,64,6,512]{3,1,2,0:T(8,128)(2,1)} %param.15) | copy-start | bytes 1179652
  10.9 29.0 %all-to-all-start = ((bf16[8,64,1152]{2,1,0:T(8,128)(2,1)}), bf16[8,64,1152]{2,1,0:T(8,128)(2,1)S(1)}, u32[]{:S(2)}, u32[]{:S(2)}) async-start(bf16[8,64,1152]{2,1,0:T(8,128)(2,1)} %get-tuple-element.27), calls=%async_computation | async-start | bytes 2359296 | tf_op jit(solution)/shard_map/all_to_all | solution.py:370
  18.6 15.8 %collective-permute-start = (bf16[2,6,1,8,512]{4,3,2,1,0:T(8,128)(2,1)S(1)}, bf16[2,6,1,8,512]{4,3,2,1,0:T(8,128)(2,1)S(1)}, u32[]{:S(2)}, u32[]{:S(2)}) collective-permute-start(bf16[2,6,1,8,512]{4,3,2,1,0:T(8,128)(2,1)S(1)} %get-tuple-element.52), channel_id=1, source_target_pairs={{0,32},{8,40},{16,48},{24,56},{32,0},{40,8},{48,16},{56,24},{1,33}... | collective-permute-start | bytes 294920 | tf_op jit(solution)/shard_map/ppermute | solution.py:332
  25.7 13.4 %collective-permute-start.1 = (bf16[2,6,1,8,512]{4,3,2,1,0:T(8,128)(2,1)S(1)}, bf16[2,6,1,8,512]{4,3,2,1,0:T(8,128)(2,1)S(1)}, u32[]{:S(2)}, u32[]{:S(2)}) collective-permute-start(bf16[2,6,1,8,512]{4,3,2,1,0:T(8,128)(2,1)S(1)} %get-tuple-element.53), channel_id=1, source_target_pairs={{0,24},{8,32},{16,40},{24,48},{32,56},{40,0},{48,8},{56,16},{1,25}... | collective-permute-start | bytes 294920 | tf_op jit(solution)/shard_map/ppermute | solution.py:332
  27.3 27.2 %collective-permute-start.2 = (bf16[2,6,1,8,512]{4,3,2,1,0:T(8,128)(2,1)S(1)}, bf16[2,6,1,8,512]{4,3,2,1,0:T(8,128)(2,1)}, u32[]{:S(2)}, u32[]{:S(2)}) collective-permute-start(bf16[2,6,1,8,512]{4,3,2,1,0:T(8,128)(2,1)S(1)} %get-tuple-element.54), channel_id=1, source_target_pairs={{0,40},{8,48},{16,56},{24,0},{32,8},{40,16},{48,24},{56,32},{1,41}... | collective-permute-start | bytes 294920 | tf_op jit(solution)/shard_map/ppermute | solution.py:332
  30.1 25.3 %collective-permute-start.3 = (bf16[2,6,1,8,512]{4,3,2,1,0:T(8,128)(2,1)S(1)}, bf16[2,6,1,8,512]{4,3,2,1,0:T(8,128)(2,1)}, u32[]{:S(2)}, u32[]{:S(2)}) collective-permute-start(bf16[2,6,1,8,512]{4,3,2,1,0:T(8,128)(2,1)S(1)} %get-tuple-element.55), channel_id=1, source_target_pairs={{0,16},{8,24},{16,32},{24,40},{32,48},{40,56},{48,0},{56,8},{1,17}... | collective-permute-start | bytes 294920 | tf_op jit(solution)/shard_map/ppermute | solution.py:332
  31.3 25.0 %collective-permute-start.4 = (bf16[2,6,1,8,512]{4,3,2,1,0:T(8,128)(2,1)S(1)}, bf16[2,6,1,8,512]{4,3,2,1,0:T(8,128)(2,1)}, u32[]{:S(2)}, u32[]{:S(2)}) collective-permute-start(bf16[2,6,1,8,512]{4,3,2,1,0:T(8,128)(2,1)S(1)} %get-tuple-element.56), channel_id=1, source_target_pairs={{0,48},{8,56},{16,0},{24,8},{32,16},{40,24},{48,32},{56,40},{1,49}... | collective-permute-start | bytes 294920 | tf_op jit(solution)/shard_map/ppermute | solution.py:332
  34.4 22.8 %collective-permute-start.5 = (bf16[2,6,1,8,512]{4,3,2,1,0:T(8,128)(2,1)}, bf16[2,6,1,8,512]{4,3,2,1,0:T(8,128)(2,1)S(1)}, u32[]{:S(2)}, u32[]{:S(2)}) collective-permute-start(bf16[2,6,1,8,512]{4,3,2,1,0:T(8,128)(2,1)} %fusion.5), channel_id=1, source_target_pairs={{0,8},{8,16},{16,24},{24,32},{32,40},{40,48},{48,56},{56,0},{1,9},... | collective-permute-start | bytes 294920 | tf_op jit(solution)/shard_map/ppermute | solution.py:332
  39.1 18.2 %collective-permute-start.6 = (bf16[2,6,1,8,512]{4,3,2,1,0:T(8,128)(2,1)S(1)}, bf16[2,6,1,8,512]{4,3,2,1,0:T(8,128)(2,1)S(1)}, u32[]{:S(2)}, u32[]{:S(2)}) collective-permute-start(bf16[2,6,1,8,512]{4,3,2,1,0:T(8,128)(2,1)S(1)} %get-tuple-element.51), channel_id=1, source_target_pairs={{0,56},{8,0},{16,8},{24,16},{32,24},{40,32},{48,40},{56,48},{1,57}... | collective-permute-start | bytes 294920 | tf_op jit(solution)/shard_map/ppermute | solution.py:332
  43.2 25.5 %all-to-all-start.1 = ((bf16[64,8,384]{2,1,0:T(8,128)(2,1)}), bf16[64,8,384]{2,1,0:T(8,128)(2,1)S(1)}, u32[]{:S(2)}, u32[]{:S(2)}) async-start(bf16[64,8,384]{2,1,0:T(8,128)(2,1)} %bitcast.6), calls=%async_computation.1 | async-start | bytes 786432 | tf_op jit(solution)/shard_map/all_to_all | solution.py:378
  54.2 80.1 %all-gather.7.cloned.1.call-start = ((), (), s32[]{:S(2)}) async-start(), calls=%async_computation.6 | async-start | bytes 3538944 | tf_op jit(solution)/shard_map/all_gather | solution.py:399
  68.8 0.7 copy-start.5
  82.9 8.8 %collective-permute-start.7 = (bf16[512,1280]{1,0:T(8,128)(2,1)}, bf16[512,1280]{1,0:T(8,128)(2,1)S(1)}, u32[]{:S(2)}, u32[]{:S(2)}) collective-permute-start(bf16[512,1280]{1,0:T(8,128)(2,1)} %get-tuple-element.30), channel_id=1, source_target_pairs={{0,64},{64,0},{128,192},{192,128},{1,65},{65,1},{129,193},{193,129... | collective-permute-start | bytes 3932168 | tf_op jit(solution)/shard_map/ppermute | solution.py:339
  87.1 20.9 %all-to-all-start.2 = ((bf16[64,8,384]{2,1,0:T(8,128)(2,1)}), bf16[64,8,384]{2,1,0:T(8,128)(2,1)S(1)}, u32[]{:S(2)}, u32[]{:S(2)}) async-start(bf16[64,8,384]{2,1,0:T(8,128)(2,1)} %bitcast.69), calls=%async_computation.2 | async-start | bytes 786432 | tf_op jit(solution)/shard_map/all_to_all | solution.py:392
  91.8 1.1 copy-start.4
  95.9 19.5 %collective-permute-start.8 = (bf16[512,640]{1,0:T(8,128)(2,1)}, bf16[512,640]{1,0:T(8,128)(2,1)}, u32[]{:S(2)}, u32[]{:S(2)}) collective-permute-start(bf16[512,640]{1,0:T(8,128)(2,1)} %constant_dynamic-slice_fusion.4), channel_id=1, source_target_pairs={{0,128},{64,192},{128,0},{192,64},{1,129},{65,193},{129,1},{193,65... | collective-permute-start | bytes 1966088 | tf_op jit(solution)/shard_map/ppermute | solution.py:339
  115.4 24.4 %all-to-all-start.3 = ((bf16[8,64,1152]{2,1,0:T(8,128)(2,1)}), bf16[8,64,1152]{2,1,0:T(8,128)(2,1)S(1)}, u32[]{:S(2)}, u32[]{:S(2)}) async-start(bf16[8,64,1152]{2,1,0:T(8,128)(2,1)} %bitcast.20), calls=%async_computation.3 | async-start | bytes 2359296 | tf_op jit(solution)/shard_map/all_to_all | solution.py:403
  127.3 2.2 %collective-permute-start.9 = (bf16[512,96]{1,0:T(8,128)(2,1)S(1)}, bf16[512,96]{1,0:T(8,128)(2,1)S(1)}, u32[]{:S(2)}, u32[]{:S(2)}) collective-permute-start(bf16[512,96]{1,0:T(8,128)(2,1)S(1)} %constant_dynamic-slice_fusion.3), channel_id=1, source_target_pairs={{0,64},{64,0},{128,192},{192,128},{1,65},{65,1},{129,193},{193,129... | collective-permute-start | bytes 294920 | tf_op jit(solution)/shard_map/ppermute | solution.py:339
  135.6 11.9 %copy-start.2 = (f32[512]{0:T(512)S(1)}, f32[512]{0:T(512)}, u32[]{:S(2)}) copy-start(f32[512]{0:T(512)} %param.9) | copy-start | bytes 6148
  135.6 12.7 %copy-start.1 = (bf16[512,1536]{1,0:T(8,128)(2,1)S(1)}, bf16[512,1536]{1,0:T(8,128)(2,1)}, u32[]{:S(2)}) copy-start(bf16[512,1536]{1,0:T(8,128)(2,1)} %w_ref.3) | copy-start | bytes 4718596
  139.8 27.8 %all-to-all-start.4 = ((bf16[64,8,736]{2,1,0:T(8,128)(2,1)}), bf16[64,8,736]{2,1,0:T(8,128)(2,1)}, u32[]{:S(2)}, u32[]{:S(2)}) async-start(bf16[64,8,736]{2,1,0:T(8,128)(2,1)} %bitcast.66), calls=%async_computation.4 | async-start | bytes 1572864 | tf_op jit(solution)/shard_map/all_to_all | solution.py:413
  179.4 2.6 %copy-start.6 = (f32[8,1536]{1,0:T(8,128)}, f32[8,1536]{1,0:T(8,128)S(1)}, u32[]{:S(2)}) copy-start(f32[8,1536]{1,0:T(8,128)S(1)} %mul.52) | copy-start | bytes 147460
Sparse Core Ops, SparseCore 0:
  11.2 79.4 all-gather.4
  92.4 41.8 all-gather.6

commit v5 on v4

--- a/solution.py
+++ b/solution.py
@@ -327,7 +327,7 @@
     me = lax.axis_index("marker")
     x = x.reshape(*lead, 6, n, 8, 512)
     out = x
-    for step in (4, 3, 5, 2, 6, 1, 7):
+    for step in (1, 7, 2, 6, 3, 5, 4):
         give = lax.dynamic_slice_in_dim(x, lax.rem(me + step, n), 1, k)
         got = lax.ppermute(give, "marker", [(i, (i + step) % n) for i in range(n)])
         out = lax.dynamic_update_slice_in_dim(out, got, lax.rem(me + n - step, n), k)

time: 190 us -> 190 us (level)
    ppermute x7, waiting for transfers between devices: 3.92 us -> 0.02 us  [to_markers(): got = lax.ppermute(give, 'marker', [(i, (i + step) % n) for i in range(n)])]
    ppermute x7, starting transfers between devices: 15.8 us -> 17.8 us  [to_markers(): got = lax.ppermute(give, 'marker', [(i, (i + step) % n) for i in range(n)])]
  transfers between devices with their start and end apart: 17 -> 17, of which waited for: 9 -> 8; matrix products, arithmetic and copies ran while one was open for 8% -> 8% of each run, Pallas kernels for 16% -> 16%
where the time goes in v5:
time: 190 us; the launch traced here: 189 us
  starting transfers between devices  60.1 us (32%)
  waiting for transfers between devices  49.3 us (26%)
  Pallas kernels  34.5 us (18%)
  between operations  14.3 us (8%)
  local copies, waits for them, and re-layouts  10.7 us (6%)
  other arithmetic  9.92 us (5%)
  blocking collectives  9.88 us (5%)
    pallas_call x6, Pallas kernels, call(): pl.pallas_call(kernel, out_shape=[jax.ShapeDtypeStruct(shape, dtype) for...  34.5 us
    ppermute x7, starting transfers between devices, to_markers(): got = lax.ppermute(give, 'marker', [(i, (i + step) % n) for i in range(n)])  17.8 us
    all_to_all x1, waiting for transfers between devices, on_device(): lax.all_to_all(shares, rows, 0, 0, tiled=True).reshape(8, 8, 8, 736)  15.7 us
    all_to_all x1, waiting for transfers between devices, on_device(): d_heads = lax.all_to_all(d_send.reshape(512, 384), both, 0, 0, tiled=True)  11.8 us
    all_to_all x1, starting transfers between devices, on_device(): got = lax.all_to_all(heads, both, 0, 0, tiled=True).reshape(8, 64, 384)  11 us
    all_to_all x1, waiting for transfers between devices, on_device(): got = lax.all_to_all(heads, both, 0, 0, tiled=True).reshape(8, 64, 384)  10.7 us
    all_gather x1, blocking collectives, on_device(): share = lax.all_gather(share, 'batch', axis=0, tiled=False)  9.88 us
    all_to_all x1, starting transfers between devices, on_device(): lax.all_to_all(shares, rows, 0, 0, tiled=True).reshape(8, 8, 8, 736)  7.64 us
  transfers between devices with their start and end apart: 17, of which 8 were waited for; matrix products, arithmetic and copies ran while one was open for 8% of the time, Pallas kernels for 16%

profile of v5, /device:TPU:1, one launch (start us, length us, event | category | flops | bytes accessed | tf_op | source)
XLA Modules:
  0.0 188.7 jit_solution(14954568380286054187)
XLA Ops:
  7.2 3.7 %shard_map.135 = (bf16[512,384]{1,0:T(8,128)(2,1)}, bf16[8,64,1152]{2,1,0:T(8,128)(2,1)}) custom-call(bf16[384,512]{1,0:T(8,128)(2,1)} %bitcast.52, f32[1,512]{1,0:T(1,128)} %bitcast.61, bf16[512,1536]{1,0:T(8,128)(2,1)} %w_ref.3), custom_call_target="tpu_custom_call" | custom-call | flops 1000000000 | bytes 4000000 | tf_op jit(solution)/shard_map/pallas_call | solution.py:311
  10.9 7.6 %all-to-all-start = ((bf16[8,64,1152]{2,1,0:T(8,128)(2,1)}), bf16[8,64,1152]{2,1,0:T(8,128)(2,1)S(1)}, u32[]{:S(2)}, u32[]{:S(2)}) async-start(bf16[8,64,1152]{2,1,0:T(8,128)(2,1)} %get-tuple-element.27), calls=%async_computation | async-start | bytes 2359296 | tf_op jit(solution)/shard_map/all_to_all | solution.py:370
  20.4 4.0 %collective-permute-start.1 = (bf16[2,6,1,8,512]{4,3,2,1,0:T(8,128)(2,1)S(1)}, bf16[2,6,1,8,512]{4,3,2,1,0:T(8,128)(2,1)S(1)}, u32[]{:S(2)}, u32[]{:S(2)}) collective-permute-start(bf16[2,6,1,8,512]{4,3,2,1,0:T(8,128)(2,1)S(1)} %get-tuple-element.53), channel_id=1, source_target_pairs={{0,56},{8,0},{16,8},{24,16},{32,24},{40,32},{48,40},{56,48},{1,57}... | collective-permute-start | bytes 294920 | tf_op jit(solution)/shard_map/ppermute | solution.py:332
  24.4 3.6 %collective-permute-start.3 = (bf16[2,6,1,8,512]{4,3,2,1,0:T(8,128)(2,1)S(1)}, bf16[2,6,1,8,512]{4,3,2,1,0:T(8,128)(2,1)}, u32[]{:S(2)}, u32[]{:S(2)}) collective-permute-start(bf16[2,6,1,8,512]{4,3,2,1,0:T(8,128)(2,1)S(1)} %get-tuple-element.55), channel_id=1, source_target_pairs={{0,48},{8,56},{16,0},{24,8},{32,16},{40,24},{48,32},{56,40},{1,49}... | collective-permute-start | bytes 294920 | tf_op jit(solution)/shard_map/ppermute | solution.py:332
  29.0 4.2 %collective-permute-start.5 = (bf16[2,6,1,8,512]{4,3,2,1,0:T(8,128)(2,1)}, bf16[2,6,1,8,512]{4,3,2,1,0:T(8,128)(2,1)S(1)}, u32[]{:S(2)}, u32[]{:S(2)}) collective-permute-start(bf16[2,6,1,8,512]{4,3,2,1,0:T(8,128)(2,1)} %fusion.5), channel_id=1, source_target_pairs={{0,40},{8,48},{16,56},{24,0},{32,8},{40,16},{48,24},{56,32},{1,41}... | collective-permute-start | bytes 294920 | tf_op jit(solution)/shard_map/ppermute | solution.py:332
  33.2 4.0 %collective-permute-start.6 = (bf16[2,6,1,8,512]{4,3,2,1,0:T(8,128)(2,1)S(1)}, bf16[2,6,1,8,512]{4,3,2,1,0:T(8,128)(2,1)S(1)}, u32[]{:S(2)}, u32[]{:S(2)}) collective-permute-start(bf16[2,6,1,8,512]{4,3,2,1,0:T(8,128)(2,1)S(1)} %get-tuple-element.51), channel_id=1, source_target_pairs={{0,32},{8,40},{16,48},{24,56},{32,0},{40,8},{48,16},{56,24},{1,33}... | collective-permute-start | bytes 294920 | tf_op jit(solution)/shard_map/ppermute | solution.py:332
  37.2 2.7 %all-to-all-done = bf16[8,64,1152]{2,1,0:T(8,128)(2,1)S(1)} async-done(((bf16[8,64,1152]{2,1,0:T(8,128)(2,1)}), bf16[8,64,1152]{2,1,0:T(8,128)(2,1)S(1)}, u32[]{:S(2)}, u32[]{:S(2)}) %all-to-all-start) | async-done | bytes 1179680 | tf_op jit(solution)/shard_map/all_to_all | solution.py:370
  39.9 3.3 %shard_map.136 = (bf16[512,384]{1,0:T(8,128)(2,1)}, f32[6,512]{1,0:T(8,128)S(1)}) custom-call(bf16[512,1152]{1,0:T(8,128)(2,1)S(1)} %bitcast.57), custom_call_target="tpu_custom_call" | custom-call | flops 2000000000 | bytes 4000000 | tf_op jit(solution)/shard_map/pallas_call | solution.py:311
  43.2 11.0 %all-to-all-start.1 = ((bf16[64,8,384]{2,1,0:T(8,128)(2,1)}), bf16[64,8,384]{2,1,0:T(8,128)(2,1)S(1)}, u32[]{:S(2)}, u32[]{:S(2)}) async-start(bf16[64,8,384]{2,1,0:T(8,128)(2,1)} %bitcast.6), calls=%async_computation.1 | async-start | bytes 786432 | tf_op jit(solution)/shard_map/all_to_all | solution.py:378
  58.2 10.7 %all-to-all-done.1 = bf16[64,8,384]{2,1,0:T(8,128)(2,1)S(1)} async-done(((bf16[64,8,384]{2,1,0:T(8,128)(2,1)}), bf16[64,8,384]{2,1,0:T(8,128)(2,1)S(1)}, u32[]{:S(2)}, u32[]{:S(2)}) %all-to-all-start.1) | async-done | bytes 393248 | tf_op jit(solution)/shard_map/all_to_all | solution.py:378
  69.7 13.4 %shard_map.137 = (bf16[512,1280]{1,0:T(8,128)(2,1)}, bf16[512,1280]{1,0:T(8,128)(2,1)}, bf16[384,512]{1,0:T(8,128)(2,1)}, bf16[8,64,384]{2,1,0:T(8,128)(2,1)}) custom-call(s32[1]{0:T(128)} %bitcast.core_ref, bf16[8,64,384]{2,1,0:T(8,128)(2,1)} %bitcast.68, bf16[384,512]{1,0:T(8,128)(2,1)} %bitcast.71, bf16[384,512]{1,0:T(8,128)(2,1)} %bitcast.70, ...), custom_call_target="tpu_custom_call" | custom-call | flops 6000000000 | bytes 4000000 | tf_op jit(solution)/shard_map/pallas_call | solution.py:311
  83.2 3.9 %collective-permute-start.7 = (bf16[512,1280]{1,0:T(8,128)(2,1)}, bf16[512,1280]{1,0:T(8,128)(2,1)S(1)}, u32[]{:S(2)}, u32[]{:S(2)}) collective-permute-start(bf16[512,1280]{1,0:T(8,128)(2,1)} %get-tuple-element.30), channel_id=1, source_target_pairs={{0,64},{64,0},{128,192},{192,128},{1,65},{65,1},{129,193},{193,129... | collective-permute-start | bytes 3932168 | tf_op jit(solution)/shard_map/ppermute | solution.py:339
  87.1 4.6 %all-to-all-start.2 = ((bf16[64,8,384]{2,1,0:T(8,128)(2,1)}), bf16[64,8,384]{2,1,0:T(8,128)(2,1)S(1)}, u32[]{:S(2)}, u32[]{:S(2)}) async-start(bf16[64,8,384]{2,1,0:T(8,128)(2,1)} %bitcast.69), calls=%async_computation.2 | async-start | bytes 786432 | tf_op jit(solution)/shard_map/all_to_all | solution.py:392
  92.8 2.0 %add_convert_fusion = bf16[512,1280]{1,0:T(8,128)(2,1)S(1)} fusion(bf16[512,1280]{1,0:T(8,128)(2,1)} %copy-done.4, bf16[512,1280]{1,0:T(8,128)(2,1)} %get-tuple-element.29), kind=kLoop, calls=%fused_computation | loop fusion | flops 2621440 | bytes 3932160 | tf_op jit(solution)/shard_map/convert_element_type | solution.py:400
  96.1 11.8 %all-to-all-done.2 = bf16[64,8,384]{2,1,0:T(8,128)(2,1)S(1)} async-done(((bf16[64,8,384]{2,1,0:T(8,128)(2,1)}), bf16[64,8,384]{2,1,0:T(8,128)(2,1)S(1)}, u32[]{:S(2)}, u32[]{:S(2)}) %all-to-all-start.2) | async-done | bytes 393248 | tf_op jit(solution)/shard_map/all_to_all | solution.py:392
  107.9 7.1 %shard_map.138.d_qkv_ref = bf16[512,1152]{1,0:T(8,128)(2,1)} custom-call(bf16[512,1152]{1,0:T(8,128)(2,1)S(1)} %bitcast.58, bf16[512,384]{1,0:T(8,128)(2,1)} %get-tuple-element.28.heads_ref, f32[6,512]{1,0:T(8,128)S(1)} %get-tuple-element.31.inv_ref, bf16[512,384]{1,0:T(8,128)(2,1)S(1)} %bitcast.59), custom_call_target="tpu_custom_call" | custom-call | flops 1000000 | bytes 10000 | tf_op jit(solution)/shard_map/pallas_call | solution.py:311
  115.3 5.7 %all-to-all-start.3 = ((bf16[8,64,1152]{2,1,0:T(8,128)(2,1)}), bf16[8,64,1152]{2,1,0:T(8,128)(2,1)S(1)}, u32[]{:S(2)}, u32[]{:S(2)}) async-start(bf16[8,64,1152]{2,1,0:T(8,128)(2,1)} %bitcast.20), calls=%async_computation.3 | async-start | bytes 2359296 | tf_op jit(solution)/shard_map/all_to_all | solution.py:403
  121.0 5.2 %shard_map.139 = bf16[512,192]{1,0:T(8,128)(2,1)} custom-call(bf16[8,512,384]{2,1,0:T(8,128)(2,1)} %bitcast.76, bf16[512,1152]{1,0:T(8,128)(2,1)} %shard_map.138.d_qkv_ref), custom_call_target="tpu_custom_call" | custom-call | flops 2000000000 | bytes 4000000 | tf_op jit(solution)/shard_map/pallas_call | solution.py:311
  130.6 3.6 %all-gather.7.cloned.1.call-done = bf16[3072,512]{1,0:T(8,128)(2,1)} async-done(((bf16[384,512]{1,0:T(8,128)(2,1)}), bf16[3072,512]{1,0:T(8,128)(2,1)}) %all-gather.7.cloned.1.call-update) | async-done | bytes 3145744 | tf_op jit(solution)/shard_map/all_gather | solution.py:399
  136.4 3.3 %all-to-all-done.3.got_ref = bf16[8,64,1152]{2,1,0:T(8,128)(2,1)S(1)} async-done(((bf16[8,64,1152]{2,1,0:T(8,128)(2,1)}), bf16[8,64,1152]{2,1,0:T(8,128)(2,1)S(1)}, u32[]{:S(2)}, u32[]{:S(2)}) %all-to-all-start.3) | async-done | bytes 1179680 | tf_op jit(solution)/shard_map/all_to_all | solution.py:403
  139.8 7.6 %all-to-all-start.4 = ((bf16[64,8,736]{2,1,0:T(8,128)(2,1)}), bf16[64,8,736]{2,1,0:T(8,128)(2,1)}, u32[]{:S(2)}, u32[]{:S(2)}) async-start(bf16[64,8,736]{2,1,0:T(8,128)(2,1)} %bitcast.66), calls=%async_computation.4 | async-start | bytes 1572864 | tf_op jit(solution)/shard_map/all_to_all | solution.py:413
  150.1 1.8 shard_map.140
  151.8 15.7 %all-to-all-done.4 = bf16[64,8,736]{2,1,0:T(8,128)(2,1)} async-done(((bf16[64,8,736]{2,1,0:T(8,128)(2,1)}), bf16[64,8,736]{2,1,0:T(8,128)(2,1)}, u32[]{:S(2)}, u32[]{:S(2)}) %all-to-all-start.4) | async-done | bytes 753696 | tf_op jit(solution)/shard_map/all_to_all | solution.py:413
  169.1 9.9 %all_gather.20 = bf16[4,8,1408]{2,1,0:T(8,128)(2,1)S(1)} all-gather(bf16[1,8,1408]{2,1,0:T(8,128)(2,1)S(1)} %pad_maximum_fusion.2), channel_id=1, replica_groups=mesh['batch'=4,'marker'=8,'space'=8] {'batch'}, dimensions={0}, use_global_device_ids=true | all-gather | bytes 112640 | tf_op jit(solution)/shard_map/all_gather | solution.py:417
  (75 shorter events, 23.9 us)
Async XLA Ops:
  7.2 100.7 %all-gather.5.cloned.1.call-start = ((), (), s32[]{:S(2)}) async-start(), calls=%async_computation.5 | async-start | bytes 3538944 | tf_op jit(solution)/shard_map/all_gather | solution.py:372
  10.9 7.6 %copy-start = (bf16[1,64,6,512]{3,1,2,0:T(8,128)(2,1)S(1)}, bf16[1,64,6,512]{3,1,2,0:T(8,128)(2,1)}, u32[]{:S(2)}) copy-start(bf16[1,64,6,512]{3,1,2,0:T(8,128)(2,1)} %param.8) | copy-start | bytes 1179652
  10.9 7.6 %copy-start.3 = (bf16[1,64,6,512]{3,1,2,0:T(8,128)(2,1)S(1)}, bf16[1,64,6,512]{3,1,2,0:T(8,128)(2,1)}, u32[]{:S(2)}) copy-start(bf16[1,64,6,512]{3,1,2,0:T(8,128)(2,1)} %param.15) | copy-start | bytes 1179652
  10.9 29.0 %all-to-all-start = ((bf16[8,64,1152]{2,1,0:T(8,128)(2,1)}), bf16[8,64,1152]{2,1,0:T(8,128)(2,1)S(1)}, u32[]{:S(2)}, u32[]{:S(2)}) async-start(bf16[8,64,1152]{2,1,0:T(8,128)(2,1)} %get-tuple-element.27), calls=%async_computation | async-start | bytes 2359296 | tf_op jit(solution)/shard_map/all_to_all | solution.py:370
  18.6 10.4 %collective-permute-start = (bf16[2,6,1,8,512]{4,3,2,1,0:T(8,128)(2,1)S(1)}, bf16[2,6,1,8,512]{4,3,2,1,0:T(8,128)(2,1)S(1)}, u32[]{:S(2)}, u32[]{:S(2)}) collective-permute-start(bf16[2,6,1,8,512]{4,3,2,1,0:T(8,128)(2,1)S(1)} %get-tuple-element.52), channel_id=1, source_target_pairs={{0,8},{8,16},{16,24},{24,32},{32,40},{40,48},{48,56},{56,0},{1,9},... | collective-permute-start | bytes 294920 | tf_op jit(solution)/shard_map/ppermute | solution.py:332
  20.4 12.8 %collective-permute-start.1 = (bf16[2,6,1,8,512]{4,3,2,1,0:T(8,128)(2,1)S(1)}, bf16[2,6,1,8,512]{4,3,2,1,0:T(8,128)(2,1)S(1)}, u32[]{:S(2)}, u32[]{:S(2)}) collective-permute-start(bf16[2,6,1,8,512]{4,3,2,1,0:T(8,128)(2,1)S(1)} %get-tuple-element.53), channel_id=1, source_target_pairs={{0,56},{8,0},{16,8},{24,16},{32,24},{40,32},{48,40},{56,48},{1,57}... | collective-permute-start | bytes 294920 | tf_op jit(solution)/shard_map/ppermute | solution.py:332
  24.4 30.1 %collective-permute-start.2 = (bf16[2,6,1,8,512]{4,3,2,1,0:T(8,128)(2,1)S(1)}, bf16[2,6,1,8,512]{4,3,2,1,0:T(8,128)(2,1)}, u32[]{:S(2)}, u32[]{:S(2)}) collective-permute-start(bf16[2,6,1,8,512]{4,3,2,1,0:T(8,128)(2,1)S(1)} %get-tuple-element.54), channel_id=1, source_target_pairs={{0,16},{8,24},{16,32},{24,40},{32,48},{40,56},{48,0},{56,8},{1,17}... | collective-permute-start | bytes 294920 | tf_op jit(solution)/shard_map/ppermute | solution.py:332
  24.4 31.0 %collective-permute-start.3 = (bf16[2,6,1,8,512]{4,3,2,1,0:T(8,128)(2,1)S(1)}, bf16[2,6,1,8,512]{4,3,2,1,0:T(8,128)(2,1)}, u32[]{:S(2)}, u32[]{:S(2)}) collective-permute-start(bf16[2,6,1,8,512]{4,3,2,1,0:T(8,128)(2,1)S(1)} %get-tuple-element.55), channel_id=1, source_target_pairs={{0,48},{8,56},{16,0},{24,8},{32,16},{40,24},{48,32},{56,40},{1,49}... | collective-permute-start | bytes 294920 | tf_op jit(solution)/shard_map/ppermute | solution.py:332
  28.0 28.3 %collective-permute-start.4 = (bf16[2,6,1,8,512]{4,3,2,1,0:T(8,128)(2,1)S(1)}, bf16[2,6,1,8,512]{4,3,2,1,0:T(8,128)(2,1)}, u32[]{:S(2)}, u32[]{:S(2)}) collective-permute-start(bf16[2,6,1,8,512]{4,3,2,1,0:T(8,128)(2,1)S(1)} %get-tuple-element.56), channel_id=1, source_target_pairs={{0,24},{8,32},{16,40},{24,48},{32,56},{40,0},{48,8},{56,16},{1,25}... | collective-permute-start | bytes 294920 | tf_op jit(solution)/shard_map/ppermute | solution.py:332
  29.0 28.2 %collective-permute-start.5 = (bf16[2,6,1,8,512]{4,3,2,1,0:T(8,128)(2,1)}, bf16[2,6,1,8,512]{4,3,2,1,0:T(8,128)(2,1)S(1)}, u32[]{:S(2)}, u32[]{:S(2)}) collective-permute-start(bf16[2,6,1,8,512]{4,3,2,1,0:T(8,128)(2,1)} %fusion.5), channel_id=1, source_target_pairs={{0,40},{8,48},{16,56},{24,0},{32,8},{40,16},{48,24},{56,32},{1,41}... | collective-permute-start | bytes 294920 | tf_op jit(solution)/shard_map/ppermute | solution.py:332
  33.2 24.0 %collective-permute-start.6 = (bf16[2,6,1,8,512]{4,3,2,1,0:T(8,128)(2,1)S(1)}, bf16[2,6,1,8,512]{4,3,2,1,0:T(8,128)(2,1)S(1)}, u32[]{:S(2)}, u32[]{:S(2)}) collective-permute-start(bf16[2,6,1,8,512]{4,3,2,1,0:T(8,128)(2,1)S(1)} %get-tuple-element.51), channel_id=1, source_target_pairs={{0,32},{8,40},{16,48},{24,56},{32,0},{40,8},{48,16},{56,24},{1,33}... | collective-permute-start | bytes 294920 | tf_op jit(solution)/shard_map/ppermute | solution.py:332
  43.2 25.8 %all-to-all-start.1 = ((bf16[64,8,384]{2,1,0:T(8,128)(2,1)}), bf16[64,8,384]{2,1,0:T(8,128)(2,1)S(1)}, u32[]{:S(2)}, u32[]{:S(2)}) async-start(bf16[64,8,384]{2,1,0:T(8,128)(2,1)} %bitcast.6), calls=%async_computation.1 | async-start | bytes 786432 | tf_op jit(solution)/shard_map/all_to_all | solution.py:378
  54.2 80.0 %all-gather.7.cloned.1.call-start = ((), (), s32[]{:S(2)}) async-start(), calls=%async_computation.6 | async-start | bytes 3538944 | tf_op jit(solution)/shard_map/all_gather | solution.py:399
  69.0 0.7 copy-start.5
  83.2 8.5 %collective-permute-start.7 = (bf16[512,1280]{1,0:T(8,128)(2,1)}, bf16[512,1280]{1,0:T(8,128)(2,1)S(1)}, u32[]{:S(2)}, u32[]{:S(2)}) collective-permute-start(bf16[512,1280]{1,0:T(8,128)(2,1)} %get-tuple-element.30), channel_id=1, source_target_pairs={{0,64},{64,0},{128,192},{192,128},{1,65},{65,1},{129,193},{193,129... | collective-permute-start | bytes 3932168 | tf_op jit(solution)/shard_map/ppermute | solution.py:339
  87.1 20.8 %all-to-all-start.2 = ((bf16[64,8,384]{2,1,0:T(8,128)(2,1)}), bf16[64,8,384]{2,1,0:T(8,128)(2,1)S(1)}, u32[]{:S(2)}, u32[]{:S(2)}) async-start(bf16[64,8,384]{2,1,0:T(8,128)(2,1)} %bitcast.69), calls=%async_computation.2 | async-start | bytes 786432 | tf_op jit(solution)/shard_map/all_to_all | solution.py:392
  91.7 1.1 copy-start.4
  95.8 19.5 %collective-permute-start.8 = (bf16[512,640]{1,0:T(8,128)(2,1)}, bf16[512,640]{1,0:T(8,128)(2,1)}, u32[]{:S(2)}, u32[]{:S(2)}) collective-permute-start(bf16[512,640]{1,0:T(8,128)(2,1)} %constant_dynamic-slice_fusion.4), channel_id=1, source_target_pairs={{0,128},{64,192},{128,0},{192,64},{1,129},{65,193},{129,1},{193,65... | collective-permute-start | bytes 1966088 | tf_op jit(solution)/shard_map/ppermute | solution.py:339
  115.3 24.4 %all-to-all-start.3 = ((bf16[8,64,1152]{2,1,0:T(8,128)(2,1)}), bf16[8,64,1152]{2,1,0:T(8,128)(2,1)S(1)}, u32[]{:S(2)}, u32[]{:S(2)}) async-start(bf16[8,64,1152]{2,1,0:T(8,128)(2,1)} %bitcast.20), calls=%async_computation.3 | async-start | bytes 2359296 | tf_op jit(solution)/shard_map/all_to_all | solution.py:403
  127.3 2.3 %collective-permute-start.9 = (bf16[512,96]{1,0:T(8,128)(2,1)S(1)}, bf16[512,96]{1,0:T(8,128)(2,1)S(1)}, u32[]{:S(2)}, u32[]{:S(2)}) collective-permute-start(bf16[512,96]{1,0:T(8,128)(2,1)S(1)} %constant_dynamic-slice_fusion.3), channel_id=1, source_target_pairs={{0,64},{64,0},{128,192},{192,128},{1,65},{65,1},{129,193},{193,129... | collective-permute-start | bytes 294920 | tf_op jit(solution)/shard_map/ppermute | solution.py:339
  135.5 12.0 %copy-start.2 = (f32[512]{0:T(512)S(1)}, f32[512]{0:T(512)}, u32[]{:S(2)}) copy-start(f32[512]{0:T(512)} %param.9) | copy-start | bytes 6148
  135.5 12.8 %copy-start.1 = (bf16[512,1536]{1,0:T(8,128)(2,1)S(1)}, bf16[512,1536]{1,0:T(8,128)(2,1)}, u32[]{:S(2)}) copy-start(bf16[512,1536]{1,0:T(8,128)(2,1)} %w_ref.3) | copy-start | bytes 4718596
  139.8 27.8 %all-to-all-start.4 = ((bf16[64,8,736]{2,1,0:T(8,128)(2,1)}), bf16[64,8,736]{2,1,0:T(8,128)(2,1)}, u32[]{:S(2)}, u32[]{:S(2)}) async-start(bf16[64,8,736]{2,1,0:T(8,128)(2,1)} %bitcast.66), calls=%async_computation.4 | async-start | bytes 1572864 | tf_op jit(solution)/shard_map/all_to_all | solution.py:413
  179.3 2.6 %copy-start.6 = (f32[8,1536]{1,0:T(8,128)}, f32[8,1536]{1,0:T(8,128)S(1)}, u32[]{:S(2)}) copy-start(f32[8,1536]{1,0:T(8,128)S(1)} %mul.52) | copy-start | bytes 147460
Sparse Core Ops, SparseCore 0:
  11.2 79.3 all-gather.4
  92.3 41.8 all-gather.6
